TPU v7x, 32 devices: a whole 2x2x4 slice. The times are simulated.
32 devices in a mesh: rep: 4 (over z), shard: 8 (over y, x, core).
Axes of the slice: x: 2, y: 2, z: 4, core: 2. Of those that a mesh axis runs over, the one named last changes fastest.
Arguments:
- tokens: bfloat16 [8192, 1024], P(('rep', 'shard')), may hold values from -6 to 6
- cotangent: bfloat16 [8192, 1024], P(('rep', 'shard')), may hold values from -6 to 6
- deal: int32 [8192], P(('rep', 'shard')), may hold values from 0 to 2047, as said below
- offsets: int32 [32, 4], P(('rep', 'shard')), may hold values from 0 to 256, as said below
- lengths: int32 [32, 4], P(('rep', 'shard')), may hold values from 0 to 256, as said below
- norm1_gain: bfloat16 [1024], P('shard'), may hold values from 0.5 to 1.5
- q_weight: bfloat16 [1024, 768], P('shard'), may hold values from -0.1875 to 0.1875
- k_weight: bfloat16 [1024, 768], P('shard'), may hold values from -0.1875 to 0.1875
- v_weight: bfloat16 [1024, 1536], P('shard'), may hold values from -0.1875 to 0.1875
- conv_weight: bfloat16 [4, 3072], P(None, 'shard'), may hold values from -3 to 3
- beta_weight: bfloat16 [1024, 6], P('shard'), may hold values from -0.1875 to 0.1875
- decay_weight: bfloat16 [1024, 6], P('shard'), may hold values from -0.1875 to 0.1875
- log_rate: float32 [6], replicated, may hold values from -6.2 to -3
- step_bias: float32 [6], replicated, may hold values from -1 to 1
- out_gate_weight: bfloat16 [1024, 1536], P('shard'), may hold values from -0.1875 to 0.1875
- out_norm_gain: bfloat16 [256], P('shard'), may hold values from 0.5 to 1.5
- out_weight: bfloat16 [1536, 1024], P('shard'), may hold values from -0.15625 to 0.15625
- norm2_gain: bfloat16 [1024], P('shard'), may hold values from 0.5 to 1.5
- ffn_gate: bfloat16 [1024, 2816], P('shard'), may hold values from -0.1875 to 0.1875
- ffn_up: bfloat16 [1024, 2816], P('shard'), may hold values from -0.1875 to 0.1875
- ffn_down: bfloat16 [2816, 1024], P('shard'), may hold values from -0.109375 to 0.109375
Outputs:
- mixed_rows: bfloat16 [8192, 1024], P(('rep', 'shard'))
- tokens_grad: bfloat16 [8192, 1024], P(('rep', 'shard'))
- norm1_gain_grad: float32 [1024], P('shard')
- q_weight_grad: float32 [1024, 768], P('shard')
- k_weight_grad: float32 [1024, 768], P('shard')
- v_weight_grad: float32 [1024, 1536], P('shard')
- conv_weight_grad: float32 [4, 3072], P(None, 'shard')
- beta_weight_grad: float32 [1024, 6], P('shard')
- decay_weight_grad: float32 [1024, 6], P('shard')
- log_rate_grad: float32 [6], replicated
- step_bias_grad: float32 [6], replicated
- out_gate_weight_grad: float32 [1024, 1536], P('shard')
- out_norm_gain_grad: float32 [256], P('shard')
- out_weight_grad: float32 [1536, 1024], P('shard')
- norm2_gain_grad: float32 [1024], P('shard')
- ffn_gate_grad: float32 [1024, 2816], P('shard')
- ffn_up_grad: float32 [1024, 2816], P('shard')
- ffn_down_grad: float32 [2816, 1024], P('shard')
Inputs may be any that keep to these rules, and one draw needn't show every extreme that they name: `deal`: within each replica's 2048 entries, a permutation of 0 to 2048 - 1 (a given row is numbered within its replica); each block takes exactly 32 rows from each device's given rows. `offsets`: per block, the first slots of up to 4 sequences: multiples of 64, not falling, the first 0; an entry equal to 256 means no sequence. `lengths`: each sequence's live tokens, from half of its slots to all of them, 0 exactly where there is no sequence; some sequence fills a whole block.
All inputs are finite; a program needn't handle non-finite values.
Results may differ from a plain program's by a relative error of at most 0.018.
Values may be sent and summed in bfloat16 or wider, within the bound.
A program may use at most 256 MiB of HBM per device.

v0:
```python
from functools import partial

import jax
import jax.numpy as jnp
from jax import lax
from jax.sharding import PartitionSpec as P

H = 6
BLOCK_LEN = 64


PRECISE_MODE = lax.Precision.HIGHEST


def shortened(array):

    def short(part):
        return part.astype(jnp.bfloat16) if part.dtype == jnp.float32 else part

    return jax.tree.map(short, array)


def rms_norm(values_in):
    return values_in * lax.rsqrt(jnp.mean(values_in * values_in, axis=-1, keepdims=True) + 1e-05)


def gained_norm(values_in, norm_gain):
    return rms_norm(values_in) * norm_gain


def silu_product(gate_in, up_in):
    return jax.nn.silu(gate_in) * up_in


def matmul_f32(left_in, right_in):
    return jnp.dot(left_in, right_in, preferred_element_type=jnp.float32)


def seq_layout(starts_in, lengths_in, row_count, block_len):
    row_index = jnp.arange(row_count, dtype=jnp.int32)
    inside = (row_index[:, None] >= starts_in[None, :]).astype(jnp.int32)
    region = jnp.sum(inside, axis=1) - 1
    picked = (region[:, None] == jnp.arange(starts_in.shape[0], dtype=jnp.int32)[None, :]).astype(
        jnp.int32
    )
    seq_begin = jnp.sum(picked * starts_in[None, :], axis=1)
    extent = jnp.sum(picked * lengths_in[None, :], axis=1)
    position = row_index - seq_begin
    live_mask = (position < extent).astype(jnp.float32)
    block_heads = jnp.arange(row_count // block_len, dtype=jnp.int32) * block_len
    resets = jnp.any(block_heads[:, None] == starts_in[None, :], axis=1).astype(jnp.float32)
    return (position, live_mask, resets)


def causal_conv(linear_in, conv_taps, position):
    row_count = linear_in.shape[0]
    summed = jnp.zeros_like(linear_in)
    for lag_step in range(conv_taps.shape[0]):
        shifted = jnp.pad(linear_in, ((lag_step, 0), (0, 0)))[:row_count]
        allowed = (position >= lag_step).astype(jnp.float32)[:, None]
        summed = summed + conv_taps[lag_step][None, :] * shifted * allowed
    return summed


def delta_rule(queries, keys_in, values_in, beta_rate, log_decay, resets, block_len):
    row_count, head_count, key_width = queries.shape
    value_width = values_in.shape[2]
    block_count = row_count // block_len

    def split_blocks(tensor):
        return tensor.reshape(block_count, block_len, head_count, -1).transpose(0, 2, 1, 3)

    query_blocks = split_blocks(queries)
    key_blocks = split_blocks(keys_in)
    value_blocks = split_blocks(values_in)
    beta_blocks = beta_rate.reshape(block_count, block_len, head_count).transpose(0, 2, 1)
    decay_blocks = log_decay.reshape(block_count, block_len, head_count).transpose(0, 2, 1)
    cumulative = jnp.cumsum(decay_blocks, axis=-1)
    lower_mask = jnp.tril(jnp.ones((block_len, block_len), jnp.float32))
    strict = lower_mask - jnp.eye(block_len, dtype=jnp.float32)
    log_gaps = cumulative[..., :, None] - cumulative[..., None, :]
    pair_decay = jnp.exp(jnp.where(lower_mask > 0, log_gaps, 0.0)) * lower_mask
    key_gram = jnp.einsum("nhid,nhjd->nhij", key_blocks, key_blocks, precision=PRECISE_MODE)
    system = (
        jnp.eye(block_len, dtype=jnp.float32)
        + beta_blocks[..., :, None] * key_gram * pair_decay * strict
    )
    right_sides = jnp.concatenate(
        [
            beta_blocks[..., None] * value_blocks,
            (beta_blocks * jnp.exp(cumulative))[..., None] * key_blocks,
        ],
        axis=-1,
    )
    solved = lax.linalg.triangular_solve(
        system, right_sides, left_side=True, lower=True, unit_diagonal=True
    )
    fresh_vals = solved[..., :value_width]
    mixing = solved[..., value_width:]
    attend = (
        jnp.einsum("nhid,nhjd->nhij", query_blocks, key_blocks, precision=PRECISE_MODE) * pair_decay
    )
    grow_decay = jnp.exp(cumulative)[..., None]
    last_cumul = cumulative[..., -1:]
    tail_decay = jnp.exp(last_cumul)[..., None]
    kscaled = key_blocks * jnp.exp(last_cumul - cumulative)[..., None]

    def advance(carried, pieces):
        q_now, fresh_now, mix_now, att_now, grow_now, tail_now, kscaled_now, reset_now = pieces
        carried = carried * (1.0 - reset_now)
        new_vals = fresh_now - jnp.einsum("hcd,hde->hce", mix_now, carried, precision=PRECISE_MODE)
        output = grow_now * jnp.einsum("hcd,hde->hce", q_now, carried, precision=PRECISE_MODE)
        output = output + jnp.einsum("hij,hje->hie", att_now, new_vals, precision=PRECISE_MODE)
        carried = tail_now * carried + jnp.einsum(
            "hcd,hce->hde", kscaled_now, new_vals, precision=PRECISE_MODE
        )
        return (carried, output)

    initial = jnp.zeros((head_count, key_width, value_width), jnp.float32)
    _, outputs = lax.scan(
        advance,
        initial,
        (query_blocks, fresh_vals, mixing, attend, grow_decay, tail_decay, kscaled, resets),
    )
    return outputs.transpose(0, 2, 1, 3).reshape(row_count, head_count, value_width)


def mixer_core(
    q_lin,
    k_lin,
    v_lin,
    gate_out_lin,
    beta_lin,
    decay_lin,
    conv_taps,
    log_rate,
    step_bias,
    norm_gain,
    position=None,
    live_mask=None,
    resets=None,
):
    row_count = q_lin.shape[0]
    key_total = q_lin.shape[1]
    key_width = key_total // H
    value_width = v_lin.shape[1] // H
    joined = jnp.concatenate([q_lin, k_lin, v_lin], axis=1)
    active = jax.nn.silu(causal_conv(joined, conv_taps, position))
    queries = active[:, :key_total].reshape(row_count, H, key_width)
    keys_in = active[:, key_total : 2 * key_total].reshape(row_count, H, key_width)
    values_in = active[:, 2 * key_total :].reshape(row_count, H, value_width)
    queries = (
        queries
        * lax.rsqrt(jnp.sum(queries * queries, axis=-1, keepdims=True) + 1e-06)
        * key_width ** (-0.5)
    )
    keys_in = keys_in * lax.rsqrt(jnp.sum(keys_in * keys_in, axis=-1, keepdims=True) + 1e-06)
    beta_rate = jax.nn.sigmoid(beta_lin) * live_mask[:, None]
    log_decay = (
        -jnp.exp(log_rate)[None, :]
        * jax.nn.softplus(decay_lin + step_bias[None, :])
        * live_mask[:, None]
    )
    heads_out = (
        delta_rule(queries, keys_in, values_in, beta_rate, log_decay, resets, BLOCK_LEN)
        * live_mask[:, None, None]
    )
    scaled = heads_out * lax.rsqrt(jnp.mean(heads_out * heads_out, axis=-1, keepdims=True) + 1e-05)
    gated = scaled * norm_gain * jax.nn.silu(gate_out_lin.reshape(row_count, H, value_width))
    return gated.reshape(row_count, H * value_width)


def local(
    tokens,
    cotangent,
    deal,
    offsets,
    lengths,
    norm1_gain,
    q_weight,
    k_weight,
    v_weight,
    conv_weight,
    beta_weight,
    decay_weight,
    log_rate,
    step_bias,
    out_gate_weight,
    out_norm_gain,
    out_weight,
    norm2_gain,
    ffn_gate,
    ffn_up,
    ffn_down,
):
    row_count = tokens.shape[0]
    model_width = tokens.shape[1]
    groups = lax.axis_size("shard")
    per_peer = row_count // groups
    source = deal // row_count
    local_row = deal % row_count
    slot_order = jnp.argsort(source, stable=True)
    wanted = local_row[slot_order].reshape(groups, per_peer)
    asked_rows = lax.all_to_all(wanted, "shard", split_axis=0, concat_axis=0, tiled=True).reshape(
        row_count
    )
    sent_x = tokens[asked_rows].reshape(groups, per_peer, model_width)
    sent_dy = cotangent[asked_rows].reshape(groups, per_peer, model_width)
    come_x, come_dy = (
        lax.all_to_all(sent_x, "shard", split_axis=0, concat_axis=0, tiled=True),
        lax.all_to_all(sent_dy, "shard", split_axis=0, concat_axis=0, tiled=True),
    )
    slot_place = jnp.argsort(slot_order)
    block_in = come_x.reshape(row_count, model_width)[slot_place]
    block_dy = come_dy.reshape(row_count, model_width)[slot_place]
    given_place = jnp.argsort(asked_rows)
    position, live_mask, resets = seq_layout(offsets[0], lengths[0], row_count, BLOCK_LEN)
    mixer_parts = (
        lax.all_gather(norm1_gain, "shard", axis=0, tiled=True),
        lax.all_gather(q_weight, "shard", axis=0, tiled=True),
        lax.all_gather(k_weight, "shard", axis=0, tiled=True),
        lax.all_gather(v_weight, "shard", axis=0, tiled=True),
        lax.all_gather(out_gate_weight, "shard", axis=0, tiled=True),
        lax.all_gather(beta_weight, "shard", axis=0, tiled=True),
        lax.all_gather(decay_weight, "shard", axis=0, tiled=True),
        lax.all_gather(out_norm_gain, "shard", axis=0, tiled=True),
        lax.all_gather(out_weight, "shard", axis=0, tiled=True),
        lax.all_gather(conv_weight, "shard", axis=1, tiled=True),
    )
    gain_one = mixer_parts[0].astype(jnp.float32)
    inputs_f = block_in.astype(jnp.float32)
    normed_in = gained_norm(inputs_f, gain_one).astype(jnp.bfloat16)
    q_lin = matmul_f32(normed_in, mixer_parts[1])
    k_lin = matmul_f32(normed_in, mixer_parts[2])
    v_lin = matmul_f32(normed_in, mixer_parts[3])
    gate_out_lin = matmul_f32(normed_in, mixer_parts[4])
    beta_lin = matmul_f32(normed_in, mixer_parts[5])
    decay_lin = matmul_f32(normed_in, mixer_parts[6])
    core_fn = partial(mixer_core, position=position, live_mask=live_mask, resets=resets)
    mixed_f, core_pull = jax.vjp(
        core_fn,
        q_lin,
        k_lin,
        v_lin,
        gate_out_lin,
        beta_lin,
        decay_lin,
        mixer_parts[9].astype(jnp.float32),
        log_rate,
        step_bias,
        mixer_parts[7].astype(jnp.float32),
    )
    mixed_out = mixed_f.astype(jnp.bfloat16)
    middle = inputs_f + matmul_f32(mixed_out, mixer_parts[8])
    ffn_parts = (
        lax.all_gather(norm2_gain, "shard", axis=0, tiled=True),
        lax.all_gather(ffn_gate, "shard", axis=0, tiled=True),
        lax.all_gather(ffn_up, "shard", axis=0, tiled=True),
        lax.all_gather(ffn_down, "shard", axis=0, tiled=True),
    )
    gain_two = ffn_parts[0].astype(jnp.float32)
    normed_mid = gained_norm(middle, gain_two).astype(jnp.bfloat16)
    gate_lin = matmul_f32(normed_mid, ffn_parts[1])
    up_lin = matmul_f32(normed_mid, ffn_parts[2])
    hidden = silu_product(gate_lin, up_lin).astype(jnp.bfloat16)
    result = (middle + matmul_f32(hidden, ffn_parts[3])).astype(jnp.bfloat16)
    ffn_parts = (
        lax.all_gather(norm2_gain, "shard", axis=0, tiled=True),
        lax.all_gather(ffn_gate, "shard", axis=0, tiled=True),
        lax.all_gather(ffn_up, "shard", axis=0, tiled=True),
        lax.all_gather(ffn_down, "shard", axis=0, tiled=True),
    )
    grad_down = matmul_f32(hidden.T, block_dy)
    grad_hidden = matmul_f32(block_dy, ffn_parts[3].T)
    _, act_pull = jax.vjp(silu_product, gate_lin, up_lin)
    grad_gate_f, grad_up_f = act_pull(grad_hidden)
    grad_gate_b = grad_gate_f.astype(jnp.bfloat16)
    grad_up_b = grad_up_f.astype(jnp.bfloat16)
    grad_ffn_gate = matmul_f32(normed_mid.T, grad_gate_b)
    grad_ffn_up = matmul_f32(normed_mid.T, grad_up_b)
    grad_normed_mid = matmul_f32(grad_gate_b, ffn_parts[1].T) + matmul_f32(
        grad_up_b, ffn_parts[2].T
    )
    _, second_pull = jax.vjp(gained_norm, middle, gain_two)
    grad_middle_n, grad_gain_two = second_pull(grad_normed_mid)
    grad_middle = block_dy.astype(jnp.float32) + grad_middle_n
    ffn_grads = (
        lax.psum_scatter(
            grad_gain_two.astype(jnp.bfloat16), "shard", scatter_dimension=0, tiled=True
        ).astype(jnp.float32),
        lax.psum_scatter(
            grad_ffn_gate.astype(jnp.bfloat16), "shard", scatter_dimension=0, tiled=True
        ).astype(jnp.float32),
        lax.psum_scatter(
            grad_ffn_up.astype(jnp.bfloat16), "shard", scatter_dimension=0, tiled=True
        ).astype(jnp.float32),
        lax.psum_scatter(
            grad_down.astype(jnp.bfloat16), "shard", scatter_dimension=0, tiled=True
        ).astype(jnp.float32),
    )
    mixer_parts = (
        lax.all_gather(norm1_gain, "shard", axis=0, tiled=True),
        lax.all_gather(q_weight, "shard", axis=0, tiled=True),
        lax.all_gather(k_weight, "shard", axis=0, tiled=True),
        lax.all_gather(v_weight, "shard", axis=0, tiled=True),
        lax.all_gather(out_gate_weight, "shard", axis=0, tiled=True),
        lax.all_gather(beta_weight, "shard", axis=0, tiled=True),
        lax.all_gather(decay_weight, "shard", axis=0, tiled=True),
        lax.all_gather(out_norm_gain, "shard", axis=0, tiled=True),
        lax.all_gather(out_weight, "shard", axis=0, tiled=True),
        lax.all_gather(conv_weight, "shard", axis=1, tiled=True),
    )
    branch_grad = grad_middle.astype(jnp.bfloat16)
    grad_out_weight = matmul_f32(mixed_out.T, branch_grad)
    grad_mixed = matmul_f32(branch_grad, mixer_parts[8].T)
    core_grads = core_pull(grad_mixed)
    grad_normed = jnp.zeros_like(inputs_f)
    weight_grads = []
    for proj_index in range(6):
        lin_grad = core_grads[proj_index].astype(jnp.bfloat16)
        weight_grads.append(matmul_f32(normed_in.T, lin_grad))
        grad_normed = grad_normed + matmul_f32(lin_grad, mixer_parts[proj_index + 1].T)
    _, first_pull = jax.vjp(gained_norm, inputs_f, gain_one)
    grad_in_n, grad_gain_one = first_pull(grad_normed)
    grad_input = (grad_middle + grad_in_n).astype(jnp.bfloat16)
    mixer_grads = (
        lax.psum_scatter(
            grad_gain_one.astype(jnp.bfloat16), "shard", scatter_dimension=0, tiled=True
        ).astype(jnp.float32),
        lax.psum_scatter(
            weight_grads[0].astype(jnp.bfloat16), "shard", scatter_dimension=0, tiled=True
        ).astype(jnp.float32),
        lax.psum_scatter(
            weight_grads[1].astype(jnp.bfloat16), "shard", scatter_dimension=0, tiled=True
        ).astype(jnp.float32),
        lax.psum_scatter(
            weight_grads[2].astype(jnp.bfloat16), "shard", scatter_dimension=0, tiled=True
        ).astype(jnp.float32),
        lax.psum_scatter(
            weight_grads[3].astype(jnp.bfloat16), "shard", scatter_dimension=0, tiled=True
        ).astype(jnp.float32),
        lax.psum_scatter(
            weight_grads[4].astype(jnp.bfloat16), "shard", scatter_dimension=0, tiled=True
        ).astype(jnp.float32),
        lax.psum_scatter(
            weight_grads[5].astype(jnp.bfloat16), "shard", scatter_dimension=0, tiled=True
        ).astype(jnp.float32),
        lax.psum_scatter(
            core_grads[9].astype(jnp.bfloat16), "shard", scatter_dimension=0, tiled=True
        ).astype(jnp.float32),
        lax.psum_scatter(
            grad_out_weight.astype(jnp.bfloat16), "shard", scatter_dimension=0, tiled=True
        ).astype(jnp.float32),
        lax.psum_scatter(
            core_grads[6].astype(jnp.bfloat16), "shard", scatter_dimension=1, tiled=True
        ).astype(jnp.float32),
    )
    decay_grads = lax.psum((core_grads[7], core_grads[8]), ("rep", "shard"))
    rep_terms = tuple(mixer_grads) + tuple(ffn_grads)
    summed = jax.tree.map(
        lambda part: part.astype(jnp.float32), lax.psum(shortened(rep_terms), "rep")
    )
    ffn_final = tuple(summed[10:14])
    rows_home = (
        lax.all_to_all(
            result[slot_order].reshape(groups, per_peer, model_width),
            "shard",
            split_axis=0,
            concat_axis=0,
            tiled=True,
        ),
        lax.all_to_all(
            grad_input[slot_order].reshape(groups, per_peer, model_width),
            "shard",
            split_axis=0,
            concat_axis=0,
            tiled=True,
        ),
    )
    mixed_rows = rows_home[0].reshape(row_count, model_width)[given_place]
    tokens_grad = rows_home[1].reshape(row_count, model_width)[given_place]
    return (
        mixed_rows,
        tokens_grad,
        summed[0],
        summed[1],
        summed[2],
        summed[3],
        summed[9],
        summed[5],
        summed[6],
        decay_grads[0],
        decay_grads[1],
        summed[4],
        summed[7],
        summed[8],
        ffn_final[0],
        ffn_final[1],
        ffn_final[2],
        ffn_final[3],
    )


def solution(mesh):
    in_specs = (
        P(("rep", "shard"), None),
        P(("rep", "shard"), None),
        P(("rep", "shard")),
        P(("rep", "shard"), None),
        P(("rep", "shard"), None),
        P("shard"),
        P("shard", None),
        P("shard", None),
        P("shard", None),
        P(None, "shard"),
        P("shard", None),
        P("shard", None),
        P(),
        P(),
        P("shard", None),
        P("shard"),
        P("shard", None),
        P("shard"),
        P("shard", None),
        P("shard", None),
        P("shard", None),
    )
    out_specs = (
        P(("rep", "shard"), None),
        P(("rep", "shard"), None),
        P("shard"),
        P("shard", None),
        P("shard", None),
        P("shard", None),
        P(None, "shard"),
        P("shard", None),
        P("shard", None),
        P(),
        P(),
        P("shard", None),
        P("shard"),
        P("shard", None),
        P("shard"),
        P("shard", None),
        P("shard", None),
        P("shard", None),
    )
    return jax.shard_map(local, mesh=mesh, in_specs=in_specs, out_specs=out_specs, check_vma=False)
```

profile of v0, /device:TPU:0, one launch (start us, length us, event | category | flops | bytes accessed | tf_op | source)
XLA Modules:
  0.0 1252.8 jit_solution(4717106204256909911)
XLA Ops:
  27.5 9.2 all-gather
  36.7 9.0 all_gather.54
  45.7 7.9 all_gather.53
  53.7 8.8 all_gather.58
  64.3 13.2 %all-reduce.16 = bf16[256]{0:T(256)(128)(2,1)S(1)} all-reduce(bf16[256]{0:T(256)(128)(2,1)S(1)} %dynamic-update-slice), channel_id=1, replica_groups=mesh['rep'=4,'shard'=8] {'shard'}, use_global_device_ids=true, to_apply=%add.16 | all-reduce | flops 256 | bytes 1024
  78.1 7.8 all-gather.1
  95.4 10.8 all-to-all-done.1
  155.1 119.3 %custom-call.7 = f32[4,6,1,64,64]{3,4,2,1,0:T(8,128)} custom-call(f32[4,6,1,64,64]{4,3,2,1,0:T(8,128)} %get-tuple-element.934), custom_call_target="InvertDiagBlocksLowerTriangular" | custom-call | tf_op jit(solution)/shard_map/jvp()/triangular_solve | solution.py:95
  289.9 51.9 %while.50 = (s32[]{:T(128)}, f32[6,128,256]{2,1,0:T(8,128)S(1)}, f32[4,6,64,256]{3,2,1,0:T(8,128)}, f32[4]{0:T(128)S(1)}, f32[4,6,128,256]{3,2,1,0:T(8,128)}, /*...) while((s32[]{:T(128)}, f32[6,128,256]{2,1,0:T(8,128)S(1)}, ...), condition=%wide.region_11.12_spmd.clone, body=%wide.region_10.11_spmd.clone.sunk | while | flops 530743296 | bytes 9055506 | solution.py:120
  372.4 6.0 fusion.217
  384.3 8.3 multiply_convert_fusion
  422.7 75.9 %while.51 = (s32[]{:T(128)}, f32[6,128,256]{2,1,0:T(8,128)S(1)}, f32[4,6,64,128]{3,2,1,0:T(8,128)}, f32[4,6,64,256]{3,2,1,0:T(8,128)}, f32[4,6,64,128]{3,2,1,0:T...) while((s32[]{:T(128)}, f32[6,128,256]{2,1,0:T(8,128)S(1)}, ...), condition=%wide.region_20.21_spmd.clone, body=%wide.region_17.20_spmd.clone.sunk | while | flops 1059618432 | bytes 27555188 | solution.py:120
  602.2 35.8 %reduce-scatter.20.cloned.1.call-done = bf16[128,768]{1,0:T(8,128)(2,1)} async-done(((bf16[1024,768]{1,0:T(8,128)(2,1)}), bf16[128,768]{1,0:T(8,128)(2,1)}) %reduce-scatter.20.cloned.1.call-update) | async-done | bytes 196624 | tf_op jit(solution)/shard_map/reduce_scatter | solution.py:333
  638.0 49.6 %reduce-scatter.22.cloned.1.call-done = bf16[128,1536]{1,0:T(8,128)(2,1)} async-done(((bf16[1024,1536]{1,0:T(8,128)(2,1)}), bf16[128,1536]{1,0:T(8,128)(2,1)}) %reduce-scatter.22.cloned.1.call-update) | async-done | bytes 393232 | tf_op jit(solution)/shard_map/reduce_scatter | solution.py:336
  687.6 49.9 %reduce-scatter.26.cloned.1.call-done = bf16[192,1024]{1,0:T(8,128)(2,1)} async-done(((bf16[1536,1024]{1,0:T(8,128)(2,1)}), bf16[192,1024]{1,0:T(8,128)(2,1)}) %reduce-scatter.26.cloned.1.call-update) | async-done | bytes 393232 | tf_op jit(solution)/shard_map/reduce_scatter | solution.py:351
  737.5 49.6 %reduce-scatter.24.cloned.1.call-done = bf16[128,1536]{1,0:T(8,128)(2,1)} async-done(((bf16[1024,1536]{1,0:T(8,128)(2,1)}), bf16[128,1536]{1,0:T(8,128)(2,1)}) %reduce-scatter.24.cloned.1.call-update) | async-done | bytes 393232 | tf_op jit(solution)/shard_map/reduce_scatter | solution.py:339
  787.1 62.8 %reduce-scatter.28.cloned.1.call-done = bf16[128,2816]{1,0:T(8,128)(2,1)} async-done(((bf16[1024,2816]{1,0:T(8,128)(2,1)}), bf16[128,2816]{1,0:T(8,128)(2,1)}) %reduce-scatter.28.cloned.1.call-update) | async-done | bytes 720912 | tf_op jit(solution)/shard_map/reduce_scatter | solution.py:291
  849.9 62.4 %reduce-scatter.30.cloned.1.call-done = bf16[128,2816]{1,0:T(8,128)(2,1)} async-done(((bf16[1024,2816]{1,0:T(8,128)(2,1)}), bf16[128,2816]{1,0:T(8,128)(2,1)}) %reduce-scatter.30.cloned.1.call-update) | async-done | bytes 720912 | tf_op jit(solution)/shard_map/reduce_scatter | solution.py:294
  912.2 62.8 %reduce-scatter.32.cloned.1.call-done = bf16[352,1024]{1,0:T(8,128)(2,1)} async-done(((bf16[2816,1024]{1,0:T(8,128)(2,1)}), bf16[352,1024]{1,0:T(8,128)(2,1)}) %reduce-scatter.32.cloned.1.call-update) | async-done | bytes 720912 | tf_op jit(solution)/shard_map/reduce_scatter | solution.py:297
  1009.0 42.9 %all-reduce.20 = (f32[6]{0:T(128)}, f32[6]{0:T(128)}) all-reduce(f32[6]{0:T(128)S(1)} %negate_multiply_fusion, f32[6]{0:T(128)S(1)} %copy-done.131), channel_id=1, replica_groups=mesh['rep'=4,'shard'=8] {'rep','shard'}, use_global_device_ids=true, to_apply=%region_52.53 | all-reduce | flops 12 | bytes 96 | tf_op jit(solution)/shard_map/psum | solution.py:358
  1051.8 13.1 %all-reduce.21 = (bf16[1024]{0:T(1024)(128)(2,1)S(1)}, bf16[256]{0:T(256)(128)(2,1)S(1)}, bf16[1024]{0:T(1024)(128)(2,1)S(1)}) all-reduce(bf16[1024]{0:T(1024)(128)(2,1)S(1)} %get-tuple-element.805, bf16[256]{0:T(256)(128)(2,1)S(1)} %copy-done.121, ...), channel_id=2, replica_groups=mesh['rep'=4,'shard'=8] {'shard'}, use_global_device_ids=true, to_apply=%region_33.34.clone | all-reduce | flops 2304 | bytes 9216
  1066.9 24.1 %reduce-scatter.34.cloned.1.call-done = bf16[384,4]{1,0:T(8,128)(2,1)} async-done(((bf16[3072,4]{1,0:T(8,128)(2,1)}), bf16[384,4]{1,0:T(8,128)(2,1)}) %reduce-scatter.34.cloned.1.call-update) | async-done | bytes 3088
  1091.9 12.1 all-reduce.22
  1111.3 125.1 %all-reduce.26.cloned.1.call-done = (bf16[128,768]{1,0:T(8,128)(2,1)}, bf16[128,768]{1,0:T(8,128)(2,1)}, bf16[128,1536]{1,0:T(8,128)(2,1)}, bf16[128,1536]{1,0:T...) async-done(((bf16[128,768]{1,0:T(8,128)(2,1)}, bf16[128,768]{1,0:T(8,128)(2,1)}, ...) | async-done | bytes 3735568 | tf_op jit(solution)/shard_map/psum | solution.py:361
  (678 shorter events, 443.5 us)
Async XLA Ops:
  7.2 114.1 %all-gather.13.cloned.1.call-start = ((), (), s32[]{:S(2)}) async-start(), calls=%async_computation.17 | async-start | bytes 1769472 | tf_op jit(solution)/shard_map/all_gather | solution.py:221
  8.0 115.4 %all-gather.11.cloned.1.call-start = ((), (), s32[]{:S(2)}) async-start(), calls=%async_computation.16 | async-start | bytes 1769472 | tf_op jit(solution)/shard_map/all_gather | solution.py:220
  8.8 117.8 %all-gather.15.cloned.1.call-start = ((), (), s32[]{:S(2)}) async-start(), calls=%async_computation.18 | async-start | bytes 3538944 | tf_op jit(solution)/shard_map/all_gather | solution.py:222
  9.5 346.4 %all-gather.17.cloned.1.call-start = ((), (), s32[]{:S(2)}) async-start(), calls=%async_computation.19 | async-start | bytes 3538944 | tf_op jit(solution)/shard_map/all_gather | solution.py:223
  10.1 357.8 %all-gather.19.cloned.1.call-start = ((), (), s32[]{:S(2)}) async-start(), calls=%async_computation.20 | async-start | bytes 3538944 | tf_op jit(solution)/shard_map/all_gather | solution.py:227
  10.7 361.7 %all-gather.21.cloned.1.call-start = ((), (), s32[]{:S(2)}) async-start(), calls=%async_computation.21 | async-start | bytes 6488064 | tf_op jit(solution)/shard_map/all_gather | solution.py:257
  11.3 367.1 %all-gather.23.cloned.1.call-start = ((), (), s32[]{:S(2)}) async-start(), calls=%async_computation.22 | async-start | bytes 6488064 | tf_op jit(solution)/shard_map/all_gather | solution.py:258
  17.9 68.7 %all-to-all-start = ((s32[8,1,32]{2,1,0:T(1,128)}), s32[8,1,32]{2,1,0:T(1,128)S(1)}, u32[]{:S(2)}, u32[]{:S(2)}) async-start(s32[8,1,32]{2,1,0:T(1,128)} %all_to_all.18), calls=%async_computation | async-start | bytes 8192 | tf_op jit(solution)/shard_map/all_to_all | solution.py:204
  23.1 361.2 %all-gather.25.cloned.1.call-start = ((), (), s32[]{:S(2)}) async-start(), calls=%async_computation.23 | async-start | bytes 6488064 | tf_op jit(solution)/shard_map/all_gather | solution.py:259
  89.8 16.4 %all-to-all-start.1 = ((bf16[8,32,1024]{2,1,0:T(8,128)(2,1)}), bf16[8,32,1024]{2,1,0:T(8,128)(2,1)S(1)}, u32[]{:S(2)}, u32[]{:S(2)}) async-start(bf16[8,32,1024]{2,1,0:T(8,128)(2,1)} %bitcast.399), calls=%async_computation.1 | async-start | bytes 1048576 | tf_op jit(solution)/shard_map/all_to_all | solution.py:210
  109.7 492.5 %reduce-scatter.18.cloned.1.call-start = ((), (), s32[]{:S(2)}) async-start(), calls=%async_computation.24 | async-start | bytes 1769472 | tf_op jit(solution)/shard_map/reduce_scatter | solution.py:330
  558.6 79.4 %reduce-scatter.20.cloned.1.call-start = ((), (), s32[]{:S(2)}) async-start(), calls=%async_computation.25 | async-start | bytes 1769472 | tf_op jit(solution)/shard_map/reduce_scatter | solution.py:333
  561.6 126.1 %reduce-scatter.22.cloned.1.call-start = ((), (), s32[]{:S(2)}) async-start(), calls=%async_computation.26 | async-start | bytes 3538944 | tf_op jit(solution)/shard_map/reduce_scatter | solution.py:336
  565.5 172.0 %reduce-scatter.26.cloned.1.call-start = ((), (), s32[]{:S(2)}) async-start(), calls=%async_computation.28 | async-start | bytes 3538944 | tf_op jit(solution)/shard_map/reduce_scatter | solution.py:351
  570.5 216.6 %reduce-scatter.24.cloned.1.call-start = ((), (), s32[]{:S(2)}) async-start(), calls=%async_computation.27 | async-start | bytes 3538944 | tf_op jit(solution)/shard_map/reduce_scatter | solution.py:339
  574.5 275.4 %reduce-scatter.28.cloned.1.call-start = ((), (), s32[]{:S(2)}) async-start(), calls=%async_computation.29 | async-start | bytes 6488064 | tf_op jit(solution)/shard_map/reduce_scatter | solution.py:291
  580.3 332.0 %reduce-scatter.30.cloned.1.call-start = ((), (), s32[]{:S(2)}) async-start(), calls=%async_computation.30 | async-start | bytes 6488064 | tf_op jit(solution)/shard_map/reduce_scatter | solution.py:294
  586.0 389.0 %reduce-scatter.32.cloned.1.call-start = ((), (), s32[]{:S(2)}) async-start(), calls=%async_computation.31 | async-start | bytes 6488064 | tf_op jit(solution)/shard_map/reduce_scatter | solution.py:297
  592.0 473.2 %reduce-scatter.36.cloned.1.call-start = ((), (), s32[]{:S(2)}) async-start(), calls=%async_computation.33 | async-start | bytes 294912
  599.5 466.5 %reduce-scatter.38.cloned.1.call-start = ((), (), s32[]{:S(2)}) async-start(), calls=%async_computation.34 | async-start | bytes 294912
  600.8 490.2 %reduce-scatter.34.cloned.1.call-start = ((), (), s32[]{:S(2)}) async-start(), calls=%async_computation.32 | async-start | bytes 884736
  602.1 634.3 %all-reduce.26.cloned.1.call-start = ((), (), s32[]{:S(2)}) async-start(), calls=%async_computation.35 | async-start | bytes 7471104 | tf_op jit(solution)/shard_map/psum | solution.py:361
  991.5 13.9 %all-to-all-start.4 = ((bf16[8,32,1024]{2,1,0:T(8,128)(2,1)}), bf16[8,32,1024]{2,1,0:T(8,128)(2,1)S(1)}, u32[]{:S(2)}, u32[]{:S(2)}) async-start(bf16[8,32,1024]{2,1,0:T(8,128)(2,1)} %bitcast.400), calls=%async_computation.4 | async-start | bytes 1048576 | tf_op jit(solution)/shard_map/all_to_all | solution.py:372
  1005.4 104.0 %all-to-all-start.2 = ((bf16[8,32,1024]{2,1,0:T(8,128)(2,1)}), bf16[8,32,1024]{2,1,0:T(8,128)(2,1)S(1)}, u32[]{:S(2)}, u32[]{:S(2)}) async-start(bf16[8,32,1024]{2,1,0:T(8,128)(2,1)} %bitcast.28), calls=%async_computation.2 | async-start | bytes 1048576 | tf_op jit(solution)/shard_map/all_to_all | solution.py:365
  (150 other events, 3297.9 us)
Sparse Core Ops, SparseCore 0:
  9.9 29.4 all-gather.12
  41.3 25.7 all-gather.10
  69.0 36.5 all-gather.14
  107.3 33.7 all-gather.16
  142.8 32.5 all-gather.18
  177.1 44.7 all-gather.20
  223.8 43.9 all-gather.22
  269.7 43.2 all-gather.24
  558.7 37.6 reduce-scatter.17
  599.5 38.4 reduce-scatter.19
  641.4 46.1 reduce-scatter.21
  691.3 46.2 reduce-scatter.25
  740.9 46.1 reduce-scatter.23
  790.8 59.0 reduce-scatter.27
  853.2 59.0 reduce-scatter.29
  915.9 59.0 reduce-scatter.31
  978.4 35.2 reduce-scatter.35
  1017.4 34.7 reduce-scatter.37
  1055.9 35.0 reduce-scatter.33
  1093.8 142.6 all-reduce.25
where the time goes:
time: 1260 us; the launch traced here: 1250 us
  waiting for transfers between devices  548 us (43%)
  matrix products  227 us (18%)
  other arithmetic  204 us (16%)
  blocking collectives  124 us (10%)
  local copies, waits for them, and re-layouts  110 us (9%)
  starting transfers between devices  20.3 us (2%)
  between operations  18.5 us (1%)
    psum x1, waiting for transfers between devices, local(): lax.psum(shortened(rep_terms), 'rep')  125 us
    another operation x4, other arithmetic, delta_rule(): lax.linalg.triangular_solve(system, right_sides, left_side=True, lower=Tr...  119 us
    dot_general x30, matrix products, matmul_f32(): return jnp.dot(left_in, right_in, preferred_element_type=jnp.float32)  96.4 us
    reduce_scatter x1, waiting for transfers between devices, local(): lax.psum_scatter(grad_ffn_gate.astype(jnp.bfloat16), 'shard', scatter_dim...  62.8 us
    reduce_scatter x1, waiting for transfers between devices, local(): lax.psum_scatter(grad_down.astype(jnp.bfloat16), 'shard', scatter_dimensi...  62.8 us
    reduce_scatter x1, waiting for transfers between devices, local(): lax.psum_scatter(grad_ffn_up.astype(jnp.bfloat16), 'shard', scatter_dimen...  62.4 us
    reduce_scatter x1, waiting for transfers between devices, local(): lax.psum_scatter(grad_out_weight.astype(jnp.bfloat16), 'shard', scatter_d...  49.9 us
    reduce_scatter x1, waiting for transfers between devices, local(): lax.psum_scatter(weight_grads[2].astype(jnp.bfloat16), 'shard', scatter_d...  49.6 us
  transfers between devices with their start and end apart: 25, of which 12 were waited for; matrix products, arithmetic and copies ran while one was open for 28% of the time, Pallas kernels for 0%

commit v1 on v0

v1 whole, which is shorter than its diff:
```python
import functools
import jax
import jax.numpy as jnp
from jax import lax
from jax.experimental import pallas as pl
from jax.experimental.pallas import tpu as pltpu
from jax.sharding import PartitionSpec as P

f32 = jnp.float32
bf16 = jnp.bfloat16
HEADS = 6
DK = 128
DVH = 256
KEYS = 768
VALS = 1536
QKV = 2 * KEYS + VALS
LANES = 128


def two_parts(a):
    hi = a.astype(bf16)
    return hi, (a - hi.astype(f32)).astype(bf16)


def dot(a, b, ca=1, cb=0):
    return lax.dot_general(a, b, (((ca,), (cb,)), ((), ())), preferred_element_type=f32)


def dot3(a, b, ca=1, cb=0):
    ah, al = a
    bh, bl = b
    return dot(ah, bh, ca, cb) + (dot(ah, bl, ca, cb) + dot(al, bh, ca, cb))


def tri_dot(tri, cols):
    hi = cols.astype(bf16)
    rest = cols - hi.astype(f32)
    mid = rest.astype(bf16)
    lo = (rest - mid.astype(f32)).astype(bf16)
    return dot(tri, hi) + (dot(tri, mid) + dot(tri, lo))


def sigm(a):
    return 1.0 / (1.0 + jnp.exp(-a))


def softplus(a):
    return jnp.maximum(a, 0.0) + jnp.log1p(jnp.exp(-jnp.abs(a)))


def layout_cols(offs, lens, n, shape, dim):
    row = lax.broadcasted_iota(jnp.int32, shape, dim)
    begin = jnp.zeros_like(row)
    extent = jnp.zeros_like(row)
    for i in range(len(offs)):
        inside = row >= offs[i]
        begin = jnp.where(inside, offs[i], begin)
        extent = jnp.where(inside, lens[i], extent)
    return begin, row - begin, (row - begin) < extent


def conv_chunk(x, taps, pos, cols):
    total = taps[0:1, cols] * x
    for t in range(1, 4):
        total = total + taps[t : t + 1, cols] * jnp.where(pos >= t, pltpu.roll(x, t, 0), 0.0)
    return total


def lane_pick(a, lane, index):
    return jnp.sum(jnp.where(lane == index, a, 0.0), axis=1, keepdims=True)


def pair_masks(n, begin_c, begin_r):
    i = lax.broadcasted_iota(jnp.int32, (n, n), 0)
    j = lax.broadcasted_iota(jnp.int32, (n, n), 1)
    same = begin_c == begin_r
    return i, j, (i >= j) & same


def mixer_forward(n, offs, lens, lin, taps, rate, bias, gain, act, cum, cum_t, tinv, fresh, heads_out, mixed):
    begin_c, pos, live = layout_cols(offs, lens, n, (n, 1), 0)
    begin_r, _, _ = layout_cols(offs, lens, n, (1, n), 1)
    live_f = live.astype(f32)
    width = 384

    def conv_step(step, carry):
        cols = pl.ds(pl.multiple_of(step * width, width), width)
        pre = conv_chunk(lin[:, cols], taps, pos, cols)
        act[:, cols] = pre * sigm(pre)
        return carry

    lax.fori_loop(0, QKV // width, conv_step, 0)
    lane = lax.broadcasted_iota(jnp.int32, (n, LANES), 1)
    bd = lin[:, QKV + VALS : QKV + VALS + LANES]
    beta = sigm(bd) * live_f
    decay = -jnp.exp(rate[...]) * softplus(bd + bias[...]) * live_f
    i, j, low = pair_masks(n, begin_c, begin_r)
    tri = (i >= j).astype(bf16)
    total = tri_dot(tri, decay)
    cum[...] = total
    cum_t[...] = total.T
    eye = (i == j).astype(f32)

    def one_head(h):
        kcols = pl.ds(pl.multiple_of(h * DK, DK), DK)
        ka = act[:, pl.ds(pl.multiple_of(KEYS + h * DK, DK), DK)]
        qa = act[:, kcols]
        vcols = pl.ds(pl.multiple_of(h * DVH, DVH), DVH)
        v = act[:, pl.ds(pl.multiple_of(2 * KEYS + h * DVH, DVH), DVH)]
        q = qa * (lax.rsqrt(jnp.sum(qa * qa, axis=1, keepdims=True) + 1e-6) * DK**-0.5)
        k = ka * lax.rsqrt(jnp.sum(ka * ka, axis=1, keepdims=True) + 1e-6)
        beta_c = lane_pick(beta, lane, h)
        cum_c = lane_pick(total, lane, HEADS + h)
        cum_r = cum_t[pl.ds(HEADS + h, 1), :]
        kk, qq = two_parts(k), two_parts(q)
        dec = jnp.where(low, jnp.exp(jnp.where(low, cum_c - cum_r, 0.0)), 0.0)
        system = jnp.where(i > j, beta_c * dot3(kk, kk, 1, 1) * dec, 0.0)
        inv = eye - jnp.where((i // 2) == (j // 2), system, 0.0)
        size = 2
        while size < n:
            off = jnp.where(((i // (2 * size)) == (j // (2 * size))) & ((i // size) != (j // size)), system, 0.0)
            parts = two_parts(inv)
            inv = inv - dot3(two_parts(dot3(parts, two_parts(off))), parts)
            size *= 2
        tinv[h] = inv
        u = dot3(two_parts(inv), two_parts(beta_c * v))
        fresh[:, vcols] = u
        o = dot3(two_parts(dot3(qq, kk, 1, 1) * dec), two_parts(u)) * live_f
        heads_out[:, vcols] = o
        gate = lin[:, pl.ds(pl.multiple_of(QKV + h * DVH, DVH), DVH)]
        scaled = o * lax.rsqrt(jnp.mean(o * o, axis=1, keepdims=True) + 1e-5)
        mixed[:, vcols] = (scaled * gain[...] * (gate * sigm(gate))).astype(bf16)

    def head_pair(step, carry):
        one_head(2 * step)
        one_head(2 * step + 1)
        return carry

    lax.fori_loop(0, HEADS // 2, head_pair, 0)


def mixer_backward(
    n, offs, lens, lin, taps, rate, bias, gain, act, cum, cum_t, tinv, fresh, heads_out, grad_mixed,
    dact, dcols, drows, lin_grad, tap_grad, gain_grad, rate_grad, bias_grad,
):
    begin_c, pos, live = layout_cols(offs, lens, n, (n, 1), 0)
    begin_r, _, _ = layout_cols(offs, lens, n, (1, n), 1)
    live_f = live.astype(f32)
    lane = lax.broadcasted_iota(jnp.int32, (n, LANES), 1)
    bd = lin[:, QKV + VALS : QKV + VALS + LANES]
    sig_b = sigm(bd)
    beta = sig_b * live_f
    i, j, low = pair_masks(n, begin_c, begin_r)
    strict = low & (i > j)
    gain_grad[...] = jnp.zeros_like(gain_grad)
    dcols[...] = jnp.zeros_like(dcols)
    drows[...] = jnp.zeros_like(drows)

    def one_head(h):
        kcols = pl.ds(pl.multiple_of(h * DK, DK), DK)
        kcols2 = pl.ds(pl.multiple_of(KEYS + h * DK, DK), DK)
        vcols = pl.ds(pl.multiple_of(h * DVH, DVH), DVH)
        vcols2 = pl.ds(pl.multiple_of(2 * KEYS + h * DVH, DVH), DVH)
        gcols = pl.ds(pl.multiple_of(QKV + h * DVH, DVH), DVH)
        ka = act[:, kcols2]
        qa = act[:, kcols]
        v = act[:, vcols2]
        o = heads_out[:, vcols]
        gate = lin[:, gcols]
        dm = grad_mixed[:, vcols]
        ro = lax.rsqrt(jnp.mean(o * o, axis=1, keepdims=True) + 1e-5)
        scaled = o * ro
        sg = sigm(gate)
        si = gate * sg
        gain_grad[...] += jnp.sum(dm * scaled * si, axis=0, keepdims=True)
        lin_grad[:, gcols] = (dm * scaled * gain[...] * (sg + si * (1.0 - sg))).astype(bf16)
        ds = dm * gain[...] * si
        d_o = two_parts(ro * (ds - scaled * jnp.mean(ds * scaled, axis=1, keepdims=True)) * live_f)
        rq = lax.rsqrt(jnp.sum(qa * qa, axis=1, keepdims=True) + 1e-6)
        rk = lax.rsqrt(jnp.sum(ka * ka, axis=1, keepdims=True) + 1e-6)
        qhat = qa * rq
        k = ka * rk
        kk, qq = two_parts(k), two_parts(qhat * DK**-0.5)
        beta_c = lane_pick(beta, lane, h)
        cum_c = lane_pick(cum[...], lane, HEADS + h)
        cum_r = cum_t[pl.ds(HEADS + h, 1), :]
        dec = jnp.where(low, jnp.exp(jnp.where(low, cum_c - cum_r, 0.0)), 0.0)
        gram = dot3(kk, kk, 1, 1)
        qk = dot3(qq, kk, 1, 1)
        uu = two_parts(fresh[:, vcols])
        du = dot3(two_parts(qk * dec), d_o, 0, 0)
        dp = dot3(d_o, uu, 1, 1) * dec
        db = dot3(two_parts(tinv[h]), two_parts(du), 0, 0)
        da = jnp.where(strict, -dot3(two_parts(db), uu, 1, 1), 0.0) * dec
        x = da * gram
        dbeta = jnp.sum(x, axis=1, keepdims=True) + jnp.sum(db * v, axis=1, keepdims=True)
        e = dp * qk + x * beta_c
        dcols[...] += jnp.where(lane == h, dbeta, 0.0) + jnp.where(
            lane == HEADS + h, jnp.sum(e, axis=1, keepdims=True), 0.0
        )
        drows[pl.ds(HEADS + h, 1), :] = jnp.sum(e, axis=0, keepdims=True)
        dact[:, vcols2] = beta_c * db
        dg = two_parts(da * beta_c)
        dpp = two_parts(dp)
        dq = dot3(dpp, kk)
        dk = dot3(dpp, qq, 0, 0) + dot3(dg, kk) + dot3(dg, kk, 0, 0)
        dact[:, kcols] = (rq * DK**-0.5) * (dq - qhat * jnp.sum(dq * qhat, axis=1, keepdims=True))
        dact[:, kcols2] = rk * (dk - k * jnp.sum(dk * k, axis=1, keepdims=True))

    def head_step(step, carry):
        one_head(2 * step)
        one_head(2 * step + 1)
        return carry

    lax.fori_loop(0, HEADS // 2, head_step, 0)

    dcum = jnp.where((lane >= HEADS) & (lane < 2 * HEADS), dcols[...] - drows[...].T, 0.0)
    ddecay = tri_dot((i <= j).astype(bf16), dcum)
    z = bd + bias[...]
    speed = -jnp.exp(rate[...]) * live_f
    dz = ddecay * speed * sigm(z)
    rate_grad[...] = jnp.sum(ddecay * speed * softplus(z), axis=0, keepdims=True)
    bias_grad[...] = jnp.sum(dz, axis=0, keepdims=True)
    dbeta_lin = dcols[...] * live_f * sig_b * (1.0 - sig_b)
    both = jnp.where(lane < HEADS, dbeta_lin, jnp.where(lane < 2 * HEADS, dz, 0.0))
    lin_grad[:, QKV + VALS : QKV + VALS + LANES] = both.astype(bf16)

    width = 384

    def conv_step(step, carry):
        cols = pl.ds(pl.multiple_of(step * width, width), width)
        x = lin[:, cols]
        pre = conv_chunk(x, taps, pos, cols)
        sg = sigm(pre)
        dc = dact[:, cols] * (sg + pre * sg * (1.0 - sg))
        dx = taps[0:1, cols] * dc
        tap_grad[0:1, cols] = jnp.sum(dc * x, axis=0, keepdims=True)
        for t in range(1, 4):
            masked = jnp.where(pos >= t, dc, 0.0)
            dx = dx + taps[t : t + 1, cols] * pltpu.roll(masked, n - t, 0)
            tap_grad[t : t + 1, cols] = jnp.sum(masked * pltpu.roll(x, t, 0), axis=0, keepdims=True)
        lin_grad[:, cols] = dx.astype(bf16)
        return carry

    lax.fori_loop(0, QKV // width, conv_step, 0)


MESH = pl.DeviceIdType.MESH


class Place:
    def __init__(self, n_shard, n_rep):
        self.n, self.reps = n_shard, n_rep
        self.ys = n_shard // 4
        self.r = lax.axis_index("rep")
        self.s = lax.axis_index("shard")
        self.c = self.s % 2
        self.x = (self.s // 2) % 2
        self.y = self.s // 4
        half = n_rep // 2
        low = self.r < half
        self.depth = jnp.where(low, self.r, n_rep - 1 - self.r)
        self.inner = jnp.where(low, self.r + 1, self.r - 1)
        self.outer = jnp.where(low, self.r - 1, self.r + 1)
        self.middle = self.depth == half - 1
        self.deep = self.depth > 0

    def shard_id(self, y, x, c):
        return (self.r, (y * 2 + x) * 2 + c)

    def core_peer(self):
        return self.shard_id(self.y, self.x, 1 - self.c)

    def x_peer(self):
        return self.shard_id(self.y, 1 - self.x, self.c)

    def y_of(self, step):
        return (self.y + step) % self.ys

    def y_peer(self, step):
        return self.shard_id(self.y_of(step), self.x, self.c)


def remote(src, dst, send, recv, device):
    return pltpu.make_async_remote_copy(
        src_ref=src, dst_ref=dst, send_sem=send, recv_sem=recv, device_id=device, device_id_type=MESH
    )


def greet(place, with_rep):
    barrier = pltpu.get_barrier_semaphore()
    n = place.n
    for step in range(1, n):
        pl.semaphore_signal(
            barrier, inc=1, device_id=(place.r, (place.s + step) % n), device_id_type=MESH
        )
    if not with_rep:
        pl.semaphore_wait(barrier, n - 1)
        return
    for step in range(1, place.reps):
        pl.semaphore_signal(
            barrier, inc=1, device_id=((place.r + step) % place.reps, place.s), device_id_type=MESH
        )
    pl.semaphore_wait(barrier, n - 1 + place.reps - 1)


def add_into(dst, idx, *others):
    total = dst[idx].astype(f32)
    for ref, at in others:
        total = total + ref[at].astype(f32)
    dst[idx] = total.astype(dst.dtype)


RING = 4


def halved(rows):
    return (rows // 2) // 16 * 16


class Ring:
    def __init__(self, n, rows, cols):
        self.n, self.rows, self.cols = n, rows, cols
        self.ys = n // 4
        self.count = 0

    def scratch(self):
        k, ys, cols = RING, self.ys, self.cols
        sems = pltpu.SemaphoreType.DMA
        per = 3 + 2 * (ys - 1)
        half = self.rows - halved(self.rows)
        return [
            pltpu.VMEM((k, ys, 2, 2, self.rows, cols), bf16),
            pltpu.VMEM((k, ys, 2, self.rows, cols), bf16),
            pltpu.VMEM((k, ys, half, cols), bf16),
            pltpu.VMEM((k, ys - 1, 2, half, cols), bf16),
            pltpu.VMEM((k, ys - 1, half, cols), bf16),
            pltpu.VMEM((k, half, cols), bf16),
            pltpu.VMEM((4, k, self.rows, cols), bf16),
            sems((k, per)),
            sems((k, per)),
            sems((k, 7)),
        ]

    def bind(self, refs):
        (self.own, self.r0, self.r1a, self.r1b, self.r2a, self.r2b, self.z, self.send, self.recv, self.zsem) = refs


class Piece:
    def __init__(self, ring, place, rows, cols, out, out_cols):
        self.ring, self.p, self.rows = ring, place, rows
        self.slot = ring.count % RING
        ring.count += 1
        self.w = pl.ds(0, cols)
        self.ra = halved(rows)
        self.rb = rows - self.ra
        self.all_rows = pl.ds(0, rows)
        self.out = out.at[:, pl.ds(out_cols, cols)]

    def own_view(self):
        return self.ring.own.at[self.slot, :, :, :, self.all_rows, self.w]

    def store_rows(self, value):
        ring = self.ring
        shaped = value.reshape(ring.ys, 2, 2, rinself.rows, value.shape[-1])
        ring.own[self.slot, :, :, :, self.all_rows, self.w] = shaped

    def send_core(self):
        g, p, k = self.ring, self.p, self.slot
        self.c0 = remote(
            g.own.at[k, :, :, 1 - p.c, self.all_rows, self.w], g.r0.at[k, :, :, self.all_rows, self.w],
            g.send.at[k, 0], g.recv.at[k, 0], p.core_peer(),
        )
        self.c0.start()

    def after_core(self):
        g, p, k, w = self.ring, self.p, self.slot, self.w
        rows = self.all_rows
        self.c0.wait()

        def step(q, carry):
            yy, xx = q // 2, q % 2
            add_into(g.own, (k, yy, xx, p.c, rows, w), (g.r0, (k, yy, xx, rows, w)))
            return carry

        lax.fori_loop(0, g.ys * 2, step, 0)
        top, low = pl.ds(0, self.ra), pl.ds(self.ra, self.rb)
        first, second = pl.ds(0, self.ra), pl.ds(0, self.rb)
        self.c1 = [
            remote(
                g.own.at[k, :, 1 - p.x, p.c, top, w], g.r1a.at[k, :, first, w],
                g.send.at[k, 1], g.recv.at[k, 1], p.x_peer(),
            )
        ]
        for d in range(1, g.ys):
            self.c1.append(
                remote(
                    g.own.at[k, p.y_of(d), :, p.c, low, w], g.r1b.at[k, d - 1, :, second, w],
                    g.send.at[k, 1 + d], g.recv.at[k, 1 + d], p.y_peer(d),
                )
            )
        for c in self.c1:
            c.start()

    def after_first(self):
        g, p, k, w = self.ring, self.p, self.slot, self.w
        top, low = pl.ds(0, self.ra), pl.ds(self.ra, self.rb)
        first, second = pl.ds(0, self.ra), pl.ds(0, self.rb)
        for c in self.c1:
            c.wait()
        for yy in range(g.ys):
            add_into(g.own, (k, yy, p.x, p.c, top, w), (g.r1a, (k, yy, first, w)))
        for xx in range(2):
            add_into(
                g.own, (k, p.y, xx, p.c, low, w),
                *[(g.r1b, (k, d, xx, second, w)) for d in range(g.ys - 1)],
            )
        self.c2 = [
            remote(
                g.own.at[k, p.y, 1 - p.x, p.c, low, w], g.r2b.at[k, second, w],
                g.send.at[k, 1 + g.ys], g.recv.at[k, 1 + g.ys], p.x_peer(),
            )
        ]
        for d in range(1, g.ys):
            self.c2.append(
                remote(
                    g.own.at[k, p.y_of(d), p.x, p.c, top, w], g.r2a.at[k, d - 1, first, w],
                    g.send.at[k, 1 + g.ys + d], g.recv.at[k, 1 + g.ys + d], p.y_peer(d),
                )
            )
        for c in self.c2:
            c.start()

    def after_second(self):
        g, p, k, w = self.ring, self.p, self.slot, self.w
        for c in self.c2:
            c.wait()
        total = g.own[k, p.y, p.x, p.c, 0 : self.ra, w].astype(f32)
        for d in range(g.ys - 1):
            total = total + g.r2a[k, d, 0 : self.ra, w].astype(f32)
        g.z[0, k, 0 : self.ra, w] = total.astype(bf16)
        total = g.own[k, p.y, p.x, p.c, self.ra : self.rows, w].astype(f32) + g.r2b[k, 0 : self.rb, w].astype(f32)
        g.z[0, k, self.ra : self.rows, w] = total.astype(bf16)
        z = lambda i: g.z.at[i, k, self.all_rows, w]
        target = lambda r: (r, p.s)
        sem = g.zsem
        self.up = remote(z(0), z(1), sem.at[k, 0], sem.at[k, 1], target(p.inner))
        self.meet = remote(z(0), z(2), sem.at[k, 2], sem.at[k, 3], target(p.inner))
        self.down = remote(z(3), z(2), sem.at[k, 4], sem.at[k, 3], target(p.outer))
        self.home = pltpu.make_async_copy(z(3), self.out, sem.at[k, 6])

        @pl.when(p.depth == 0)
        def _():
            self.send_inward()

    def send_inward(self):
        p = self.p

        @pl.when(p.middle)
        def _():
            self.meet.start()

        @pl.when(jnp.logical_not(p.middle))
        def _():
            self.up.start()

    def after_up(self):
        g, p, k, w = self.ring, self.p, self.slot, self.w

        @pl.when(p.deep)
        def _():
            self.up.wait_recv()
            add_into(g.z, (0, k, self.all_rows, w), (g.z, (1, k, self.all_rows, w)))
            self.send_inward()

    def finish(self, middle):
        g, p, k, w = self.ring, self.p, self.slot, self.w
        rows = self.all_rows

        @pl.when(p.middle if middle else jnp.logical_not(p.middle))
        def _():
            self.meet.wait_recv()
            if middle:
                both = g.z[0, k, rows, w].astype(f32) + g.z[2, k, rows, w].astype(f32)
                g.z[3, k, rows, w] = both.astype(bf16)
            else:
                g.z[3, k, rows, w] = g.z[2, k, rows, w]

            @pl.when(p.deep)
            def _():
                self.down.start()

            self.home.start()

    def close(self):
        p = self.p

        @pl.when(p.middle)
        def _():
            self.meet.wait_send()

        @pl.when(jnp.logical_not(p.middle))
        def _():
            self.up.wait_send()

        @pl.when(p.deep)
        def _():
            self.down.wait_send()

        self.home.wait()


def pump(pieces, index):
    stages = [
        (7, lambda q: q.close()),
        (6, lambda q: q.finish(False)),
        (5, lambda q: q.finish(True)),
        (4, lambda q: q.after_up()),
        (3, lambda q: q.after_second()),
        (2, lambda q: q.after_first()),
        (1, lambda q: q.after_core()),
    ]
    for lag, act in stages:
        if 0 <= index - lag < len(pieces):
            act(pieces[index - lag])


class Small:
    def __init__(self, n, reps, rows, cols):
        self.n, self.ys, self.reps = n, n // 4, reps
        self.sizes = (2, 2, self.ys, reps)
        self.rows, self.cols = rows, cols

    def scratch(self):
        total = sum(self.sizes)
        return [
            pltpu.VMEM((total, self.rows, self.cols), f32),
            pltpu.SemaphoreType.DMA((total,)),
            pltpu.SemaphoreType.DMA((total,)),
        ]

    def bind(self, refs):
        self.buf, self.send, self.recv = refs

    def begin(self, place, axis, value):
        base = sum(self.sizes[:axis])
        size = self.sizes[axis]
        p = place
        mine = (p.c, p.x, p.y, p.r)[axis]
        slot = self.buf.at[base + mine]
        slot[...] = value
        self.copies = []
        for d in range(1, size):
            at = (mine + d) % size
            device = (
                p.shard_id(p.y, p.x, at), p.shard_id(p.y, at, p.c), p.shard_id(at, p.x, p.c), (at, p.s),
            )[axis]
            self.copies.append(remote(slot, slot, self.send.at[base + d], self.recv.at[base + d], device))
        for c in self.copies:
            c.start()

    def end(self, axis):
        base = sum(self.sizes[:axis])
        for c in self.copies:
            c.wait()
        total = self.buf[base]
        for d in range(1, self.sizes[axis]):
            total = total + self.buf[base + d]
        return total


def columns(total, widths):
    cuts, at = [], 0
    while at < total:
        width = next(w for w in widths if w <= total - at)
        cuts.append((at, width))
        at += width
    return cuts


FFN_CUTS = ((0, 768), (768, 768), (1536, 640), (2176, 640))


def scatter_kernel(n, reps, rings, small, *refs):
    gg, gu, gd, go, gp, small_in = refs[:6]
    og, ou, od, oo, oq, ok, ov, ot, ob, small_out = refs[6:16]
    rest = refs[16:]
    ring_a, ring_b = rings
    load_sem = rest[0]
    rest = rest[1:]
    ring_a.bind(rest[:10])
    ring_b.bind(rest[10:20])
    small.bind(rest[20:23])
    place = Place(n, reps)
    greet(place, True)
    pieces = []
    loads = []
    rows_a = gg.shape[3]

    def add(ring, rows, cols, src, src_at, out, out_at):
        piece = Piece(ring, place, rows, cols, out, out_at)
        src_view = src.at[:, :, :, :, pl.ds(src_at, cols)]
        pieces.append(piece)
        loads.append(pltpu.make_async_copy(src_view, piece.own_view(), load_sem.at[len(pieces) % 2]))

    for src, out in ((gg, og), (gu, ou)):
        for at, width in FFN_CUTS:
            add(ring_a, rows_a, width, src, at, out, at)
    for at in range(0, 1024, 256):
        add(ring_b, gd.shape[3], 256, gd, at, od, at)
    for at in range(0, 1024, 256):
        add(ring_b, go.shape[3], 256, go, at, oo, at)
    at = 0
    for out in (oq, ok, ov, ot, ob):
        for inner, width in columns(out.shape[1], (768, 128)):
            add(ring_a, rows_a, width, gp, at, out, inner)
            at += width
    value = small_in[...]
    for index in range(len(pieces) + 7):
        if index < 4:
            small.begin(place, index, value)
        pump(pieces, index)
        if index < len(pieces):
            loads[index].start()
            loads[index].wait()
            pieces[index].send_core()
        if index < 4:
            value = small.end(index)
    small_out[...] = value


def scatter_sums(n, reps, gg, gu, gd, go, gp, small_in):
    rings = (Ring(n, gg.shape[0] // n, 768), Ring(n, gd.shape[0] // n, 256))
    small = Small(n, reps, *small_in.shape)
    anywhere = pl.BlockSpec(memory_space=pl.ANY)
    held = pl.BlockSpec(memory_space=pltpu.VMEM)
    rows = gg.shape[0] // n

    def shards(g):
        return g.reshape(n // 4, 2, 2, g.shape[0] // n, g.shape[1])

    shape = lambda r, c: jax.ShapeDtypeStruct((r, c), bf16)
    outs = [
        shape(rows, gg.shape[1]), shape(rows, gu.shape[1]), shape(gd.shape[0] // n, gd.shape[1]),
        shape(go.shape[0] // n, go.shape[1]), shape(rows, KEYS), shape(rows, KEYS), shape(rows, VALS),
        shape(rows, VALS), shape(rows, LANES), jax.ShapeDtypeStruct(small_in.shape, f32),
    ]
    return pl.pallas_call(
        functools.partial(scatter_kernel, n, reps, rings, small),
        out_shape=outs,
        in_specs=[anywhere] * 5 + [held],
        out_specs=[anywhere] * 9 + [held],
        scratch_shapes=[pltpu.SemaphoreType.DMA((2,))] + rings[0].scratch() + rings[1].scratch() + small.scratch(),
        compiler_params=pltpu.CompilerParams(collective_id=0, has_side_effects=True, vmem_limit_bytes=60 << 20),
    )(shards(gg), shards(gu), shards(gd), shards(go), shards(gp), small_in)


def forward_call(n, offs, lens, lin, taps, rate, bias, gain):
    held = pl.BlockSpec(memory_space=pltpu.VMEM)
    words = pl.BlockSpec(memory_space=pltpu.SMEM)

    def kernel(offs, lens, *refs):
        count = offs.shape[0]
        mixer_forward(n, [offs[i] for i in range(count)], [lens[i] for i in range(count)], *refs)

    sd = lambda s, d=f32: jax.ShapeDtypeStruct(s, d)
    return pl.pallas_call(
        kernel,
        in_specs=[words, words] + [held] * 5,
        out_specs=[held] * 7,
        out_shape=[sd((n, QKV)), sd((n, LANES)), sd((LANES, n)), sd((HEADS, n, n)), sd((n, VALS)), sd((n, VALS)), sd((n, VALS), bf16)],
        compiler_params=pltpu.CompilerParams(vmem_limit_bytes=56 << 20),
    )(offs, lens, lin, taps, rate, bias, gain)


def backward_call(n, offs, lens, lin, taps, rate, bias, gain, saved, grad_mixed):
    held = pl.BlockSpec(memory_space=pltpu.VMEM)
    words = pl.BlockSpec(memory_space=pltpu.SMEM)

    def kernel(offs, lens, *refs):
        count = offs.shape[0]
        mixer_backward(n, [offs[i] for i in range(count)], [lens[i] for i in range(count)], *refs)

    sd = lambda s, d=f32: jax.ShapeDtypeStruct(s, d)
    wide = QKV + VALS + LANES
    return pl.pallas_call(
        kernel,
        in_specs=[words, words] + [held] * 12,
        out_specs=[held] * 8,
        out_shape=[sd((n, QKV)), sd((n, LANES)), sd((LANES, n)), sd((n, wide), bf16), sd((4, QKV)), sd((1, DVH)), sd((1, LANES)), sd((1, LANES))],
        compiler_params=pltpu.CompilerParams(vmem_limit_bytes=56 << 20),
    )(offs, lens, lin, taps, rate, bias, gain, *saved, grad_mixed)


def mm(a, b):
    return jnp.dot(a, b, preferred_element_type=f32)


def local(
    reps, tokens, cotangent, deal, offsets, lengths, norm1_gain, q_weight, k_weight, v_weight, conv_weight,
    beta_weight, decay_weight, log_rate, step_bias, out_gate_weight, out_norm_gain, out_weight, norm2_gain,
    ffn_gate, ffn_up, ffn_down,
):
    rows, width = tokens.shape
    n = lax.axis_size("shard")
    per_peer = rows // n
    source = deal // rows
    local_row = deal % rows
    slot_order = jnp.argsort(source, stable=True)
    wanted = local_row[slot_order].reshape(n, per_peer)
    swap = functools.partial(lax.all_to_all, axis_name="shard", split_axis=0, concat_axis=0, tiled=True)
    asked = swap(wanted).reshape(rows)
    slot_place = jnp.argsort(slot_order)
    block_in = swap(tokens[asked].reshape(n, per_peer, width)).reshape(rows, width)[slot_place]
    block_dy = swap(cotangent[asked].reshape(n, per_peer, width)).reshape(rows, width)[slot_place]
    given_place = jnp.argsort(asked)
    gather = functools.partial(lax.all_gather, axis_name="shard", axis=0, tiled=True)
    pad = LANES - 2 * HEADS
    bd_weight = jnp.concatenate([beta_weight, decay_weight, jnp.zeros((beta_weight.shape[0], pad), bf16)], axis=1)
    proj = [gather(w) for w in (q_weight, k_weight, v_weight, out_gate_weight, bd_weight)]
    gain1, gain2, gain_o = [gather(g).astype(f32)[None, :] for g in (norm1_gain, norm2_gain, out_norm_gain)]
    taps = lax.all_gather(conv_weight, "shard", axis=1, tiled=True).astype(f32)
    w_out, w_gate, w_up, w_down = [gather(w) for w in (out_weight, ffn_gate, ffn_up, ffn_down)]
    lanes = lambda a: jnp.pad(a, (HEADS, LANES - 2 * HEADS))[None, :]
    rate, bias = lanes(log_rate), lanes(step_bias)

    x = block_in.astype(f32)
    r1 = lax.rsqrt(jnp.mean(x * x, axis=-1, keepdims=True) + 1e-5)
    normed_in = (x * r1 * gain1).astype(bf16)
    lin = jnp.concatenate([mm(normed_in, w) for w in proj], axis=1)
    saved = forward_call(rows, offsets[0], lengths[0], lin, taps, rate, bias, gain_o)
    mixed = saved[6]
    middle = x + mm(mixed, w_out)
    r2 = lax.rsqrt(jnp.mean(middle * middle, axis=-1, keepdims=True) + 1e-5)
    normed_mid = (middle * r2 * gain2).astype(bf16)
    gate, up = mm(normed_mid, w_gate), mm(normed_mid, w_up)
    sg = jax.nn.sigmoid(gate)
    hidden = (gate * sg * up).astype(bf16)
    result = (middle + mm(hidden, w_down)).astype(bf16)
    grad_down = mm(hidden.T, block_dy).astype(bf16)
    grad_hidden = mm(block_dy, w_down.T)
    grad_gate = (grad_hidden * up * (sg + gate * sg * (1.0 - sg))).astype(bf16)
    grad_up = (grad_hidden * gate * sg).astype(bf16)
    g_gate = mm(normed_mid.T, grad_gate).astype(bf16)
    g_up = mm(normed_mid.T, grad_up).astype(bf16)
    gnm = mm(grad_gate, w_gate.T) + mm(grad_up, w_up.T)
    g_norm2 = jnp.sum(gnm * middle * r2, axis=0)
    u = gnm * gain2
    grad_middle = block_dy.astype(f32) + r2 * (u - middle * (r2 * r2) * jnp.mean(u * middle, axis=-1, keepdims=True))
    branch = grad_middle.astype(bf16)
    g_out = mm(mixed.T, branch).astype(bf16)
    grad_mixed = mm(branch, w_out.T)
    back = backward_call(rows, offsets[0], lengths[0], lin, taps, rate, bias, gain_o, saved[:6], grad_mixed)
    lin_grad = back[3]
    g_proj = mm(normed_in.T, lin_grad).astype(bf16)
    grad_normed = mm(lin_grad, jnp.concatenate(proj, axis=1).T)
    g_norm1 = jnp.sum(grad_normed * x * r1, axis=0)
    u = grad_normed * gain1
    grad_in = (grad_middle + r1 * (u - x * (r1 * r1) * jnp.mean(u * x, axis=-1, keepdims=True))).astype(bf16)

    flat = jnp.concatenate([back[5][0], back[6][0], back[7][0]])
    small = jnp.concatenate(
        [
            back[4].reshape(-1, width), g_norm1[None], g_norm2[None],
            jnp.pad(flat, (0, width - flat.shape[0]))[None], jnp.zeros((1, width), f32),
        ],
        axis=0,
    )
    sums = scatter_sums(n, reps, g_gate, g_up, grad_down, g_out, g_proj, small)
    small = sums[9]
    s = lax.axis_index("shard")

    def part(a, dim=0):
        size = a.shape[dim] // n
        return lax.dynamic_slice_in_dim(a, s * size, size, dim)

    home = lambda a: swap(a[slot_order].reshape(n, per_peer, width)).reshape(rows, width)[given_place]
    f = lambda a: a.astype(f32)
    bd = sums[8]
    return (
        home(result), home(grad_in), part(small[12]), f(sums[4]), f(sums[5]), f(sums[6]),
        part(small[:12].reshape(4, QKV), 1), f(bd[:, :HEADS]), f(bd[:, HEADS : 2 * HEADS]),
        small[14, DVH + HEADS : DVH + 2 * HEADS], small[14, DVH + LANES + HEADS : DVH + LANES + 2 * HEADS],
        f(sums[7]), part(small[14, :DVH]), f(sums[3]), part(small[13]), f(sums[0]), f(sums[1]), f(sums[2]),
    )


def solution(mesh):
    rows2, shard0 = P(("rep", "shard"), None), P("shard", None)
    vec = P("shard")
    in_specs = (
        rows2, rows2, P(("rep", "shard")), rows2, rows2, vec, shard0, shard0, shard0, P(None, "shard"),
        shard0, shard0, P(), P(), shard0, vec, shard0, vec, shard0, shard0, shard0,
    )
    out_specs = (
        rows2, rows2, vec, shard0, shard0, shard0, P(None, "shard"), shard0, shard0, P(), P(), shard0,
        vec, shard0, vec, shard0, shard0, shard0,
    )
    body = functools.partial(local, mesh.shape["rep"])
    return jax.shard_map(body, mesh=mesh, in_specs=in_specs, out_specs=out_specs, check_vma=False)
```

time: 1260 us -> 618 us (0.49)
  waiting for transfers between devices: 548 us -> 133 us
  Pallas kernels: 0 us -> 242 us
  other arithmetic: 204 us -> 22.7 us
  matrix products: 227 us -> 77.8 us
  local copies, waits for them, and re-layouts: 110 us -> 39.6 us
  blocking collectives: 124 us -> 62.9 us
    reduce_scatter x8 -> x0, waiting for transfers between devices: 373 us -> none  [the longest x1 62.8 us: local(): lax.psum_scatter(grad_ffn_gate.astype(jnp.bfloat16), 'shard', scatter_dim...]
    pallas_call x0 -> x3, Pallas kernels: none -> 242 us  [the longest x1 178 us: scatter_sums(): pl.pallas_call(functools.partial(scatter_kernel, n, reps, rings, small),...]
    dot_general x85 -> x19, matrix products: 218 us -> 77.8 us  [mm(): return jnp.dot(a, b, preferred_element_type=f32)]
    psum x1 -> x0, waiting for transfers between devices: 125 us -> none  [local(): lax.psum(shortened(rep_terms), 'rep')]
    all_gather x8, waiting for transfers between devices: 0.05 us -> 125 us  [local(): gather(w)]
    another operation x8 -> x0, other arithmetic: 124 us -> none  [the longest x4 119 us: delta_rule(): lax.linalg.triangular_solve(system, right_sides, left_side=True, lower=Tr...]
    psum x2 -> x0, blocking collectives: 55 us -> none  [the longest x1 42.9 us: local(): decay_grads = lax.psum((core_grads[7], core_grads[8]), ('rep', 'shard'))]
    reduce_sum x23 -> x1, other arithmetic: 24.9 us -> 0.18 us  [local(): r1 = lax.rsqrt(jnp.mean(x * x, axis=-1, keepdims=True) + 1e-05)]
  transfers between devices with their start and end apart: 25 -> 12, of which waited for: 12 -> 5; matrix products, arithmetic and copies ran while one was open for 28% -> 14% of each run, Pallas kernels for 0% -> 35%
where the time goes in v1:
time: 618 us; the launch traced here: 609 us
  Pallas kernels  242 us (39%)
  waiting for transfers between devices  133 us (22%)
  matrix products  77.8 us (13%)
  blocking collectives  62.9 us (10%)
  local copies, waits for them, and re-layouts  39.6 us (6%)
  other arithmetic  22.7 us (4%)
  between operations  15.8 us (3%)
  starting transfers between devices  14.5 us (2%)
    pallas_call x1, Pallas kernels, scatter_sums(): pl.pallas_call(functools.partial(scatter_kernel, n, reps, rings, small),...  178 us
    all_gather x8, waiting for transfers between devices, local(): gather(w)  125 us
    dot_general x19, matrix products, mm(): return jnp.dot(a, b, preferred_element_type=f32)  77.8 us
    pallas_call x1, Pallas kernels, forward_call(): pl.pallas_call(kernel, in_specs=[words, words] + [held] * 5, out_specs=[h...  36.2 us
    pallas_call x1, Pallas kernels, backward_call(): pl.pallas_call(kernel, in_specs=[words, words] + [held] * 12, out_specs=[...  27.7 us
    all_gather x2, blocking collectives, local(): gather(g).astype(f32)[None, :]  15.4 us
    all_gather x1, blocking collectives, local(): gather(w)  15.4 us
    unnamed x91, local copies, waits for them, and re-layouts  14.3 us
  transfers between devices with their start and end apart: 12, of which 5 were waited for; matrix products, arithmetic and copies ran while one was open for 14% of the time, Pallas kernels for 35%

profile of v1, /device:TPU:0, one launch (start us, length us, event | category | flops | bytes accessed | tf_op | source)
XLA Modules:
  0.0 608.8 jit_solution(14158168225045013296)
XLA Ops:
  18.0 9.7 %all_to_all.29 = s32[8,1,32]{2,1,0:T(1,128)S(1)} all-to-all(s32[8,1,32]{2,1,0:T(1,128)S(1)} %all_to_all.18), channel_id=1, replica_groups=mesh['rep'=4,'shard'=8] {'shard'}, dimensions={0} | all-to-all | bytes 2048 | tf_op jit(solution)/shard_map/all_to_all | solution.py:712
  47.7 15.4 %all_gather.44 = bf16[1024,128]{1,0:T(8,128)(2,1)S(1)} all-gather(bf16[128,128]{1,0:T(8,128)(2,1)S(1)} %maximum_maximum_fusion), channel_id=1, replica_groups=mesh['rep'=4,'shard'=8] {'shard'}, dimensions={0}, use_global_device_ids=true | all-gather | bytes 294912 | tf_op jit(solution)/shard_map/all_gather | solution.py:720
  63.1 7.7 %all-gather = bf16[8,1,128]{2,1,0:T(2,128)(2,1)S(1)} all-gather(bf16[1,1,128]{2,1,0:T(2,128)(2,1)S(1)} %bitcast.107), channel_id=1, replica_groups=mesh['rep'=4,'shard'=8] {'shard'}, dimensions={0}, use_global_device_ids=true | all-gather | bytes 2304 | tf_op jit(solution)/shard_map/all_gather | solution.py:721
  72.3 13.3 %all-reduce.3 = bf16[256]{0:T(256)(128)(2,1)S(1)} all-reduce(bf16[256]{0:T(256)(128)(2,1)S(1)} %dynamic-update-slice), channel_id=1, replica_groups=mesh['rep'=4,'shard'=8] {'shard'}, use_global_device_ids=true, to_apply=%add.3 | all-reduce | flops 256 | bytes 1024
  86.2 9.0 %all_gather.45 = bf16[4,3072]{1,0:T(4,128)(2,1)S(1)} all-gather(bf16[4,384]{1,0:T(4,128)(2,1)S(1)} %copy-done.23), channel_id=1, replica_groups=mesh['rep'=4,'shard'=8] {'shard'}, dimensions={1}, use_global_device_ids=true | all-gather | bytes 27648 | tf_op jit(solution)/shard_map/all_gather | solution.py:722
  95.8 7.7 %all-gather.1 = bf16[8,1,128]{2,1,0:T(2,128)(2,1)S(1)} all-gather(bf16[1,1,128]{2,1,0:T(2,128)(2,1)S(1)} %bitcast.108), channel_id=1, replica_groups=mesh['rep'=4,'shard'=8] {'shard'}, dimensions={0}, use_global_device_ids=true | all-gather | bytes 2304 | tf_op jit(solution)/shard_map/all_gather | solution.py:721
  118.2 4.1 convolution_dynamic-update-slice_fusion.1
  122.4 17.5 %all-gather.17.cloned.1.call-done = bf16[1024,1536]{1,0:T(8,128)(2,1)} async-done(((bf16[128,1536]{1,0:T(8,128)(2,1)}), bf16[1024,1536]{1,0:T(8,128)(2,1)}) %all-gather.17.cloned.1.call-update) | async-done | bytes 3145744 | tf_op jit(solution)/shard_map/all_gather | solution.py:720
  139.9 4.1 convolution_dynamic-update-slice_fusion
  145.0 36.2 %shard_map.340 = (f32[256,3072]{1,0:T(8,128)}, f32[256,128]{1,0:T(8,128)}, f32[128,256]{1,0:T(8,128)}, f32[6,256,256]{2,1,0:T(8,128)}, f32[256,1536]{1,0:T(8,128...) custom-call(s32[4]{0:T(128)} %bitcast.102, s32[4]{0:T(128)} %bitcast.104, ...), custom_call_target="tpu_custom_call" | custom-call | tf_op jit(solution)/shard_map/pallas_call | solution.py:667
  190.3 28.7 %all-gather.21.cloned.1.call-done = bf16[1024,2816]{1,0:T(8,128)(2,1)} async-done(((bf16[128,2816]{1,0:T(8,128)(2,1)}), bf16[1024,2816]{1,0:T(8,128)(2,1)}) %all-gather.21.cloned.1.call-update) | async-done | bytes 5767184 | tf_op jit(solution)/shard_map/all_gather | solution.py:723
  219.1 5.9 fusion.28
  225.0 39.3 %all-gather.23.cloned.1.call-done = bf16[1024,2816]{1,0:T(8,128)(2,1)} async-done(((bf16[128,2816]{1,0:T(8,128)(2,1)}), bf16[1024,2816]{1,0:T(8,128)(2,1)}) %all-gather.23.cloned.1.call-update) | async-done | bytes 5767184 | tf_op jit(solution)/shard_map/all_gather | solution.py:723
  264.3 5.8 fusion.29
  270.2 39.4 %all-gather.25.cloned.1.call-done = bf16[2816,1024]{1,0:T(8,128)(2,1)} async-done(((bf16[352,1024]{1,0:T(8,128)(2,1)}), bf16[2816,1024]{1,0:T(8,128)(2,1)}) %all-gather.25.cloned.1.call-update) | async-done | bytes 5767184 | tf_op jit(solution)/shard_map/all_gather | solution.py:723
  309.6 9.1 %multiply_convert_fusion = (bf16[256,2816]{1,0:T(8,128)(2,1)S(1)}, bf16[256,2816]{1,0:T(8,128)(2,1)S(1)}, bf16[256,2816]{1,0:T(8,128)(2,1)}) fusion(f32[256,2816]{1,0:T(8,128)} %fusion.28, f32[256,2816]{1,0:T(8,128)} %fusion.29, bf16[256,1024]{1,0:T(8,128)(2,1)S(1)} %gather_fusion.6, bf16[2816,1024]{1,0:T(8,128)(2,1)} %all-gather.25.cloned.1.call-done), kind=kOutput, calls=%fused_computation.16 | convolution fusion | flops 1487208448 | bytes 16384000 | tf_op jit(solution)/shard_map/dot_general | solution.py:696
  318.6 4.1 convolution_convert_fusion.3
  322.8 4.2 convolution_convert_fusion.2
  336.7 27.7 %shard_map.341 = (f32[256,3072]{1,0:T(8,128)}, f32[256,128]{1,0:T(8,128)}, f32[128,256]{1,0:T(8,128)}, bf16[256,4736]{1,0:T(8,128)(2,1)}, f32[4,3072]{1,0:T(4,12...) custom-call(s32[4]{0:T(128)} %bitcast.103, s32[4]{0:T(128)} %bitcast.105, ...), custom_call_target="tpu_custom_call" | custom-call | tf_op jit(solution)/shard_map/pallas_call | solution.py:686
  364.4 7.3 %convolution_convert_fusion = bf16[1024,4736]{1,0:T(8,128)(2,1)} fusion(bf16[256,4736]{1,0:T(8,128)(2,1)} %get-tuple-element.53, bf16[256,1024]{1,0:T(8,128)(2,1)S(1)} %gather_fusion.2, f32[1024]{0:T(1024)S(1)} %bitcast.88, f32[256]{0:T(256)S(1)} %get-tuple-element.136), kind=kOutput, calls=%fused_computation.9 | convolution fusion | flops 2488926208 | bytes 12653568 | tf_op jit(solution)/shard_map/dot_general | solution.py:696
  371.7 7.5 %fusion.12 = (f32[1024]{0:T(1024)S(1)}, f32[256]{0:T(256)S(1)}, f32[256,1024]{1,0:T(8,128)}) fusion(bf16[256,1024]{1,0:T(8,128)(2,1)S(1)} %gather_fusion.2, f32[256]{0:T(256)S(1)} %get-tuple-element.136, f32[1024]{0:T(1024)S(1)} %bitcast.89, bf16[256,4736]{1,0:T(8,128)(2,1)S(1)} %copy-done.9, bf16[1024,4736]{1,0:T(8,128)(2,1)} %constant_dynamic-update-slice_fusion), kind=kOutput, calls=%fused_computation.43 | convolution fusion | flops 2484861696 | bytes 13707264 | tf_op jit(solution)/shard_map/dot_general | solution.py:696
  379.9 5.6 convolution_convert_fusion.1
  391.7 4.3 fusion.1
  400.1 178.0 %shard_map.342 = (bf16[128,2816]{1,0:T(8,128)(2,1)}, bf16[128,2816]{1,0:T(8,128)(2,1)}, bf16[352,1024]{1,0:T(8,128)(2,1)}, bf16[192,1024]{1,0:T(8,128)(2,1)}, bf...) custom-call(bf16[2,2,2,128,2816]{4,3,2,1,0:T(8,128)(2,1)} %bitcast.8, ...), custom_call_target="tpu_custom_call" | custom-call | tf_op jit(solution)/shard_map/pallas_call | solution.py:648
  (196 shorter events, 101.0 us)
Async XLA Ops:
  7.2 21.8 %copy-start = (bf16[256,1024]{1,0:T(8,128)(2,1)S(1)}, bf16[256,1024]{1,0:T(8,128)(2,1)}, u32[]{:S(2)}) copy-start(bf16[256,1024]{1,0:T(8,128)(2,1)} %param.21) | copy-start | bytes 1572868
  7.2 102.2 %all-gather.11.cloned.1.call-start = ((), (), s32[]{:S(2)}) async-start(), calls=%async_computation.5 | async-start | bytes 1769472 | tf_op jit(solution)/shard_map/all_gather | solution.py:720
  8.0 104.3 %all-gather.13.cloned.1.call-start = ((), (), s32[]{:S(2)}) async-start(), calls=%async_computation.6 | async-start | bytes 1769472 | tf_op jit(solution)/shard_map/all_gather | solution.py:720
  8.7 109.5 %all-gather.15.cloned.1.call-start = ((), (), s32[]{:S(2)}) async-start(), calls=%async_computation.7 | async-start | bytes 3538944 | tf_op jit(solution)/shard_map/all_gather | solution.py:720
  9.4 130.4 %all-gather.17.cloned.1.call-start = ((), (), s32[]{:S(2)}) async-start(), calls=%async_computation.8 | async-start | bytes 3538944 | tf_op jit(solution)/shard_map/all_gather | solution.py:720
  10.0 177.2 %all-gather.19.cloned.1.call-start = ((), (), s32[]{:S(2)}) async-start(), calls=%async_computation.9 | async-start | bytes 3538944 | tf_op jit(solution)/shard_map/all_gather | solution.py:723
  10.6 208.5 %all-gather.21.cloned.1.call-start = ((), (), s32[]{:S(2)}) async-start(), calls=%async_computation.10 | async-start | bytes 6488064 | tf_op jit(solution)/shard_map/all_gather | solution.py:723
  11.2 253.2 %all-gather.23.cloned.1.call-start = ((), (), s32[]{:S(2)}) async-start(), calls=%async_computation.11 | async-start | bytes 6488064 | tf_op jit(solution)/shard_map/all_gather | solution.py:723
  11.9 297.6 %all-gather.25.cloned.1.call-start = ((), (), s32[]{:S(2)}) async-start(), calls=%async_computation.12 | async-start | bytes 6488064 | tf_op jit(solution)/shard_map/all_gather | solution.py:723
  17.8 16.6 %copy-start.32 = (f32[6]{0:T(128)S(1)}, f32[6]{0:T(128)}, u32[]{:S(2)}) copy-start(f32[6]{0:T(128)} %param.34) | copy-start | bytes 76
  17.9 16.6 %copy-start.33 = (f32[6]{0:T(128)S(1)}, f32[6]{0:T(128)}, u32[]{:S(2)}) copy-start(f32[6]{0:T(128)} %param.33) | copy-start | bytes 76
  17.9 20.4 %copy-start.24 = (bf16[128,6]{0,1:T(8,128)(2,1)S(1)}, bf16[128,6]{0,1:T(8,128)(2,1)}, u32[]{:S(2)}) copy-start(bf16[128,6]{0,1:T(8,128)(2,1)} %param.31) | copy-start | bytes 4612
  17.9 20.6 %copy-start.25 = (bf16[128,6]{0,1:T(8,128)(2,1)S(1)}, bf16[128,6]{0,1:T(8,128)(2,1)}, u32[]{:S(2)}) copy-start(bf16[128,6]{0,1:T(8,128)(2,1)} %param.32) | copy-start | bytes 4612
  17.9 20.9 %copy-start.2 = (bf16[256,1024]{1,0:T(8,128)(2,1)S(1)}, bf16[256,1024]{1,0:T(8,128)(2,1)}, u32[]{:S(2)}) copy-start(bf16[256,1024]{1,0:T(8,128)(2,1)} %param.22) | copy-start | bytes 1572868
  31.0 13.2 %all-to-all-start.1 = ((bf16[8,32,1024]{2,1,0:T(8,128)(2,1)}), bf16[8,32,1024]{2,1,0:T(8,128)(2,1)S(1)}, u32[]{:S(2)}, u32[]{:S(2)}) async-start(bf16[8,32,1024]{2,1,0:T(8,128)(2,1)} %bitcast.1), calls=%async_computation.1 | async-start | bytes 1048576 | tf_op jit(solution)/shard_map/all_to_all | solution.py:714
  34.5 28.6 %copy-start.28 = (bf16[128]{0:T(256)(128)(2,1)S(1)}, bf16[128]{0:T(256)(128)(2,1)}, u32[]{:S(2)}) copy-start(bf16[128]{0:T(256)(128)(2,1)} %param.26) | copy-start | bytes 772
  34.5 36.3 %copy-start.35 = (u32[32]{0:T(128)S(1)}, u32[32]{0:T(128)}, u32[]{:S(2)}) copy-start(u32[32]{0:T(128)} %constant.74) | copy-start | bytes 388
  34.5 37.5 %copy-start.34 = (bf16[32]{0:T(256)(128)(2,1)S(1)}, bf16[32]{0:T(256)(128)(2,1)}, u32[]{:S(2)}) copy-start(bf16[32]{0:T(256)(128)(2,1)} %param.36) | copy-start | bytes 196
  34.5 51.6 %copy-start.23 = (bf16[4,384]{1,0:T(4,128)(2,1)S(1)}, bf16[4,384]{1,0:T(4,128)(2,1)}, u32[]{:S(2)}) copy-start(bf16[4,384]{1,0:T(4,128)(2,1)} %param.30) | copy-start | bytes 9220
  38.7 57.2 %copy-start.29 = (bf16[128]{0:T(256)(128)(2,1)S(1)}, bf16[128]{0:T(256)(128)(2,1)}, u32[]{:S(2)}) copy-start(bf16[128]{0:T(256)(128)(2,1)} %param.38) | copy-start | bytes 772
  44.2 63.8 %all-to-all-start.3 = ((bf16[8,32,1024]{2,1,0:T(8,128)(2,1)}), bf16[8,32,1024]{2,1,0:T(8,128)(2,1)S(1)}, u32[]{:S(2)}, u32[]{:S(2)}) async-start(bf16[8,32,1024]{2,1,0:T(8,128)(2,1)} %bitcast.15), calls=%async_computation.3 | async-start | bytes 1048576 | tf_op jit(solution)/shard_map/all_to_all | solution.py:715
  144.0 37.2 %copy-start.3 = (bf16[1024,1536]{1,0:T(8,128)(2,1)S(1)}, bf16[1024,1536]{1,0:T(8,128)(2,1)}, u32[]{:S(2)}) copy-start(bf16[1024,1536]{1,0:T(8,128)(2,1)} %all-gather.15.cloned.1.call-done) | copy-start | bytes 9437188
  387.9 192.5 %all-to-all-start.4 = ((bf16[8,32,1024]{2,1,0:T(8,128)(2,1)}), bf16[8,32,1024]{2,1,0:T(8,128)(2,1)S(1)}, u32[]{:S(2)}, u32[]{:S(2)}) async-start(bf16[8,32,1024]{2,1,0:T(8,128)(2,1)} %bitcast.17), calls=%async_computation.4 | async-start | bytes 1048576 | tf_op jit(solution)/shard_map/all_to_all | solution.py:777
  580.4 19.1 %all-to-all-start.2 = ((bf16[8,32,1024]{2,1,0:T(8,128)(2,1)}), bf16[8,32,1024]{2,1,0:T(8,128)(2,1)S(1)}, u32[]{:S(2)}, u32[]{:S(2)}) async-start(bf16[8,32,1024]{2,1,0:T(8,128)(2,1)} %bitcast.13), calls=%async_computation.2 | async-start | bytes 1048576 | tf_op jit(solution)/shard_map/all_to_all | solution.py:777
  (28 other events, 132.8 us)
Sparse Core Ops, SparseCore 0:
  9.9 28.4 all-gather.10
  40.3 30.8 all-gather.12
  73.1 32.3 all-gather.14
  107.3 32.5 all-gather.16
  141.6 32.3 all-gather.18
  175.7 43.3 all-gather.20
  221.0 43.3 all-gather.22
  266.2 43.3 all-gather.24

commit v2 on v1

--- a/solution.py
+++ b/solution.py
@@ -89,17 +89,18 @@
         act[:, cols] = pre * sigm(pre)
         return carry
 
-    lax.fori_loop(0, QKV // width, conv_step, 0)
     lane = lax.broadcasted_iota(jnp.int32, (n, LANES), 1)
     bd = lin[:, QKV + VALS : QKV + VALS + LANES]
     beta = sigm(bd) * live_f
     decay = -jnp.exp(rate[...]) * softplus(bd + bias[...]) * live_f
     i, j, low = pair_masks(n, begin_c, begin_r)
-    tri = (i >= j).astype(bf16)
-    total = tri_dot(tri, decay)
-    cum[...] = total
-    cum_t[...] = total.T
     eye = (i == j).astype(f32)
+
+    def convolve():
+        lax.fori_loop(0, QKV // width, conv_step, 0)
+        total = tri_dot((i >= j).astype(bf16), decay)
+        cum[...] = total
+        cum_t[...] = total.T
 
     def one_head(h):
         kcols = pl.ds(pl.multiple_of(h * DK, DK), DK)
@@ -110,7 +111,7 @@
         q = qa * (lax.rsqrt(jnp.sum(qa * qa, axis=1, keepdims=True) + 1e-6) * DK**-0.5)
         k = ka * lax.rsqrt(jnp.sum(ka * ka, axis=1, keepdims=True) + 1e-6)
         beta_c = lane_pick(beta, lane, h)
-        cum_c = lane_pick(total, lane, HEADS + h)
+        cum_c = lane_pick(cum[...], lane, HEADS + h)
         cum_r = cum_t[pl.ds(HEADS + h, 1), :]
         kk, qq = two_parts(k), two_parts(q)
         dec = jnp.where(low, jnp.exp(jnp.where(low, cum_c - cum_r, 0.0)), 0.0)
@@ -131,12 +132,14 @@
         scaled = o * lax.rsqrt(jnp.mean(o * o, axis=1, keepdims=True) + 1e-5)
         mixed[:, vcols] = (scaled * gain[...] * (gate * sigm(gate))).astype(bf16)
 
-    def head_pair(step, carry):
-        one_head(2 * step)
-        one_head(2 * step + 1)
-        return carry
-
-    lax.fori_loop(0, HEADS // 2, head_pair, 0)
+    def pair(step):
+        def run():
+            one_head(2 * step)
+            one_head(2 * step + 1)
+
+        return run
+
+    return [convolve] + [pair(step) for step in range(HEADS // 2)]
 
 
 def mixer_backward(
@@ -152,9 +155,11 @@
     beta = sig_b * live_f
     i, j, low = pair_masks(n, begin_c, begin_r)
     strict = low & (i > j)
-    gain_grad[...] = jnp.zeros_like(gain_grad)
-    dcols[...] = jnp.zeros_like(dcols)
-    drows[...] = jnp.zeros_like(drows)
+
+    def clear():
+        gain_grad[...] = jnp.zeros_like(gain_grad)
+        dcols[...] = jnp.zeros_like(dcols)
+        drows[...] = jnp.zeros_like(drows)
 
     def one_head(h):
         kcols = pl.ds(pl.multiple_of(h * DK, DK), DK)
@@ -207,23 +212,17 @@
         dact[:, kcols] = (rq * DK**-0.5) * (dq - qhat * jnp.sum(dq * qhat, axis=1, keepdims=True))
         dact[:, kcols2] = rk * (dk - k * jnp.sum(dk * k, axis=1, keepdims=True))
 
-    def head_step(step, carry):
-        one_head(2 * step)
-        one_head(2 * step + 1)
-        return carry
-
-    lax.fori_loop(0, HEADS // 2, head_step, 0)
-
-    dcum = jnp.where((lane >= HEADS) & (lane < 2 * HEADS), dcols[...] - drows[...].T, 0.0)
-    ddecay = tri_dot((i <= j).astype(bf16), dcum)
-    z = bd + bias[...]
-    speed = -jnp.exp(rate[...]) * live_f
-    dz = ddecay * speed * sigm(z)
-    rate_grad[...] = jnp.sum(ddecay * speed * softplus(z), axis=0, keepdims=True)
-    bias_grad[...] = jnp.sum(dz, axis=0, keepdims=True)
-    dbeta_lin = dcols[...] * live_f * sig_b * (1.0 - sig_b)
-    both = jnp.where(lane < HEADS, dbeta_lin, jnp.where(lane < 2 * HEADS, dz, 0.0))
-    lin_grad[:, QKV + VALS : QKV + VALS + LANES] = both.astype(bf16)
+    def rates():
+        dcum = jnp.where((lane >= HEADS) & (lane < 2 * HEADS), dcols[...] - drows[...].T, 0.0)
+        ddecay = tri_dot((i <= j).astype(bf16), dcum)
+        z = bd + bias[...]
+        speed = -jnp.exp(rate[...]) * live_f
+        dz = ddecay * speed * sigm(z)
+        rate_grad[...] = jnp.sum(ddecay * speed * softplus(z), axis=0, keepdims=True)
+        bias_grad[...] = jnp.sum(dz, axis=0, keepdims=True)
+        dbeta_lin = dcols[...] * live_f * sig_b * (1.0 - sig_b)
+        both = jnp.where(lane < HEADS, dbeta_lin, jnp.where(lane < 2 * HEADS, dz, 0.0))
+        lin_grad[:, QKV + VALS : QKV + VALS + LANES] = both.astype(bf16)
 
     width = 384
 
@@ -242,7 +241,12 @@
         lin_grad[:, cols] = dx.astype(bf16)
         return carry
 
-    lax.fori_loop(0, QKV // width, conv_step, 0)
+    def convolve(first, last):
+        return lambda: lax.fori_loop(first, last, conv_step, 0)
+
+    heads = [functools.partial(one_head, h) for h in range(HEADS)]
+    total = QKV // width
+    return clear, heads, rates, [convolve(0, total // 2), convolve(total // 2, total)]
 
 
 MESH = pl.DeviceIdType.MESH
@@ -569,131 +573,726 @@
         return total
 
 
-def columns(total, widths):
-    cuts, at = [], 0
-    while at < total:
-        width = next(w for w in widths if w <= total - at)
-        cuts.append((at, width))
-        at += width
-    return cuts
-
-
-FFN_CUTS = ((0, 768), (768, 768), (1536, 640), (2176, 640))
-
-
-def scatter_kernel(n, reps, rings, small, *refs):
-    gg, gu, gd, go, gp, small_in = refs[:6]
-    og, ou, od, oo, oq, ok, ov, ot, ob, small_out = refs[6:16]
-    rest = refs[16:]
+class Flow:
+    COUNT = staticmethod(lambda ys: 3 + 6 * (ys - 1))
+
+    def __init__(self, place, src, src_at, cols, dst, dst_at, send, recv, base, mine):
+        self.p, self.rows = place, src.shape[0]
+        self.src = src.at[:, pl.ds(src_at, cols)]
+        self.dst, self.cols = dst, pl.ds(dst_at, cols)
+        self.send, self.recv, self.base, self.used = send, recv, base, 0
+        self.ra = halved(self.rows)
+        self.mine = pltpu.make_async_copy(self.src, self.region(place.y, place.x, place.c), mine)
+        self.all = []
+
+    def region(self, y, x, c, half=None):
+        start = ((y * 2 + x) * 2 + c) * self.rows
+        size = self.rows
+        if half == 0:
+            size = self.ra
+        elif half == 1:
+            start, size = start + self.ra, self.rows - self.ra
+        return self.dst.at[pl.ds(pl.multiple_of(start, 16), size), self.cols]
+
+    def copy(self, dst, device, src=None):
+        at = self.base + self.used
+        self.used += 1
+        c = remote(dst if src is None else src, dst, self.send.at[at], self.recv.at[at], device)
+        c.start()
+        self.all.append(c)
+        return c
+
+    def begin(self):
+        p = self.p
+        own = self.region(p.y, p.x, p.c)
+        self.mine.start()
+        self.from_x = self.copy(own, p.x_peer(), self.src)
+        self.from_y = [self.copy(own, p.y_peer(d), self.src) for d in range(1, p.ys)]
+        self.from_core = [self.copy(own, p.core_peer(), self.src)]
+
+    def forward(self):
+        p = self.p
+        steps = range(1, p.ys)
+        self.from_x.wait_recv()
+        self.diag = [self.copy(self.region(p.y, 1 - p.x, p.c, 0), p.y_peer(d)) for d in steps]
+        self.from_core.append(self.copy(self.region(p.y, 1 - p.x, p.c), p.core_peer()))
+        for d in steps:
+            self.from_y[d - 1].wait_recv()
+            back = p.y_of(p.ys - d)
+            self.diag.append(self.copy(self.region(back, p.x, p.c, 1), p.x_peer()))
+            self.from_core.append(self.copy(self.region(back, p.x, p.c), p.core_peer()))
+
+    def relay(self):
+        p = self.p
+        for i, c in enumerate(self.diag):
+            c.wait_recv()
+            half, d = divmod(i, p.ys - 1)
+            back = p.y_of(p.ys - d - 1)
+            self.from_core.append(self.copy(self.region(back, 1 - p.x, p.c, half), p.core_peer()))
+
+    def done(self):
+        for c in self.from_core:
+            c.wait_recv()
+        self.mine.wait()
+
+    def close(self):
+        for c in self.all:
+            c.wait_send()
+
+
+FF_SPLIT = 1536
+FTILE = 256
+
+
+def one_hot_rows(values, count):
+    return lax.broadcasted_iota(jnp.int32, (count, values.shape[1]), 0) == values
+
+
+class Store:
+    def __init__(self, sem):
+        self.sem, self.all = sem, []
+
+    def put(self, src, dst):
+        c = pltpu.make_async_copy(src, dst, self.sem.at[len(self.all)])
+        c.start()
+        self.all.append(c)
+
+    def wait(self):
+        for c in self.all:
+            c.wait()
+
+
+FORWARD_SAVED = (
+    ("xin", lambda n, d, f: ((n, d), bf16)),
+    ("dy", lambda n, d, f: ((n, d), bf16)),
+    ("normed_t", lambda n, d, f: ((d, n), bf16)),
+    ("lin", lambda n, d, f: ((n, QKV + VALS + LANES), f32)),
+    ("act", lambda n, d, f: ((n, QKV), f32)),
+    ("cum", lambda n, d, f: ((n, LANES), f32)),
+    ("cum_t", lambda n, d, f: ((LANES, n), f32)),
+    ("tinv", lambda n, d, f: ((HEADS, n, n), f32)),
+    ("fresh", lambda n, d, f: ((n, VALS), f32)),
+    ("heads", lambda n, d, f: ((n, VALS), f32)),
+    ("mixed_t", lambda n, d, f: ((VALS, n), bf16)),
+    ("middle", lambda n, d, f: ((n, d), f32)),
+    ("normed_mid_t", lambda n, d, f: ((d, n), bf16)),
+    ("hidden", lambda n, d, f: ((n, f), bf16)),
+    ("hidden_t", lambda n, d, f: ((f, n), bf16)),
+    ("grads_gu", lambda n, d, f: ((n, 2 * f), bf16)),
+    ("pick", lambda n, d, f: ((n, n), bf16)),
+    ("place", lambda n, d, f: ((n, n), bf16)),
+    ("params", lambda n, d, f: ((16, d), f32)),
+    ("taps", lambda n, d, f: ((4, QKV), f32)),
+)
+
+
+def transposed(a):
+    return a.T.astype(bf16)
+
+
+def forward_kernel(n_shard, reps, *refs):
+    take = iter(refs)
+    get = lambda k: [next(take) for _ in range(k)]
+    offs, lens, tokens, cot, deal, small_in, rate, bias = get(8)
+    wq, wk, wv, wt, wb, wo, wg, wu, wd = get(9)
+    gp, go, gg, gu, gd = get(5)
+    outs = dict(zip([name for name, _ in FORWARD_SAVED], get(len(FORWARD_SAVED))))
+    kept = dict(zip([name for name, _ in FORWARD_SAVED], get(len(FORWARD_SAVED))))
+    (dealt, dsend, drecv, smalls, ssend, srecv, sent, come, tsend, trecv, wbuf, wobuf, wdbuf, load_sem, fsend, frecv,
+     mine_sem, out_sem, normed, mixed, normed_mid) = get(21)
+    rows, width = tokens.shape
+    per = rows // n_shard
+    place = Place(n_shard, reps)
+    p = place
+    greet(place, False)
+    offsets = [offs[i] for i in range(offs.shape[0])]
+    lengths = [lens[i] for i in range(lens.shape[0])]
+    store = Store(out_sem)
+
+    dealt[p.s] = deal[...]
+    smalls[p.s] = small_in[...]
+    first = []
+    for d in range(1, n_shard):
+        to = (p.r, (p.s + d) % n_shard)
+        first.append(remote(dealt.at[p.s], dealt.at[p.s], dsend.at[d], drecv.at[d], to))
+        first[-1].start()
+    for d in range(1, n_shard):
+        to = (p.r, (p.s + d) % n_shard)
+        first.append(remote(smalls.at[p.s], smalls.at[p.s], ssend.at[d], srecv.at[d], to))
+        first[-1].start()
+
+    per_flow = Flow.COUNT(p.ys)
+    made = []
+
+    def flow(src, at, cols, dst, dst_at):
+        k = len(made)
+        made.append(Flow(place, src, at, cols, dst, dst_at, fsend, frecv, k * per_flow, mine_sem.at[k]))
+        return made[-1]
+
+    ff = wg.shape[1]
+    stages = [
+        [flow(wq, 0, KEYS, gp, 0), flow(wk, 0, KEYS, gp, KEYS)],
+        [flow(wv, 0, VALS, gp, 2 * KEYS)],
+        [flow(wt, 0, VALS, gp, QKV), flow(wb, 0, LANES, gp, QKV + VALS)],
+        [flow(wo, 0, width, go, 0)],
+        [flow(wd, 0, width // 2, gd, 0)],
+        [flow(wd, width // 2, width // 2, gd, width // 2)],
+        [flow(wg, 0, FF_SPLIT, gg, 0)],
+        [flow(wu, 0, FF_SPLIT, gu, 0)],
+        [flow(wg, FF_SPLIT, ff - FF_SPLIT, gg, FF_SPLIT)],
+        [flow(wu, FF_SPLIT, ff - FF_SPLIT, gu, FF_SPLIT)],
+    ]
+
+    def advance(k):
+        for lag, act in ((0, "begin"), (2, "forward"), (3, "relay"), (4, "done")):
+            if 0 <= k - lag < len(stages):
+                for f in stages[k - lag]:
+                    getattr(f, act)()
+
+    loads = {}
+
+    def load(name, src, dst):
+        loads[name] = pltpu.make_async_copy(src, dst, load_sem.at[len(loads)])
+        loads[name].start()
+
+    for c in first[: n_shard - 1]:
+        c.wait_recv()
+    i = lax.broadcasted_iota(jnp.int32, (rows, rows), 0)
+    j = lax.broadcasted_iota(jnp.int32, (rows, rows), 1)
+    upper = (i <= j).astype(bf16)
+    everyone = dealt[:, 0, :]
+    to_me = (everyone // rows) == p.s
+    rank = dot(to_me.astype(f32).astype(bf16), upper).astype(jnp.int32) - 1
+    rank = jnp.where(to_me, rank, -1)
+    for b in range(n_shard):
+        picked = one_hot_rows(rank[b : b + 1, :], per).astype(f32).astype(bf16)
+        which = one_hot_rows(everyone[b : b + 1, :] % rows, rows).astype(f32).astype(bf16)
+        kept["pick"][b * per : (b + 1) * per, :] = dot(picked, which, 1, 1).astype(bf16)
+    pick = kept["pick"][...]
+    exchange = []
+    for a, src in enumerate((tokens, cot)):
+        for at in range(0, width, 256):
+            sent[a, :, at : at + 256] = dot(pick, src[:, at : at + 256]).astype(bf16)
+        for d in range(1, n_shard):
+            t = (p.s + d) % n_shard
+            exchange.append(
+                remote(
+                    sent.at[a, pl.ds(pl.multiple_of(t * per, 16), per)],
+                    come.at[a, pl.ds(pl.multiple_of(p.s * per, 16), per)],
+                    tsend.at[a, d], trecv.at[a, d], (p.r, t),
+                )
+            )
+            exchange[-1].start()
+        if a == 0:
+            advance(0)
+            advance(1)
+        here = pl.ds(pl.multiple_of(p.s * per, 16), per)
+        come[a, here, :] = sent[a, here, :]
+    mine = deal[0:1, :]
+    source = mine // rows
+    from_each = one_hot_rows(source, n_shard)
+    cum = dot(from_each.astype(f32).astype(bf16), upper)
+    slot = jnp.sum(jnp.where(from_each, cum, 0.0), axis=0, keepdims=True).astype(jnp.int32) - 1 + source * per
+    kept["place"][...] = one_hot_rows(slot, rows).astype(f32).astype(bf16)
+    store.put(kept["pick"], outs["pick"])
+    store.put(kept["place"], outs["place"])
+
+    for c in first[n_shard - 1 :]:
+        c.wait_recv()
+    total = smalls[0].astype(f32)
+    for t in range(1, n_shard):
+        total = total + smalls[t].astype(f32)
+    kept["params"][...] = total
+    for t in range(4):
+        for g in range(QKV // width):
+            row = t * (QKV // width) + g
+            kept["taps"][t : t + 1, g * width : (g + 1) * width] = total[row : row + 1, :]
+    gain1, gain2 = kept["params"].at[12:13, :], kept["params"].at[13:14, :]
+    gain_o = kept["params"].at[14:15, 0:DVH]
+    store.put(kept["params"], outs["params"])
+    store.put(kept["taps"], outs["taps"])
+
+    for a, name in enumerate(("xin", "dy")):
+        for c in exchange[a * (n_shard - 1) : (a + 1) * (n_shard - 1)]:
+            c.wait_recv()
+        for at in range(0, width, 256):
+            kept[name][:, at : at + 256] = dot(kept["place"][...], come[a, :, at : at + 256], 0, 0).astype(bf16)
+        store.put(kept[name], outs[name])
+    x = kept["xin"][...].astype(f32)
+    norm = x * lax.rsqrt(jnp.mean(x * x, axis=1, keepdims=True) + 1e-5) * gain1[...]
+    normed[...] = norm.astype(bf16)
+    kept["normed_t"][...] = transposed(norm)
+    store.put(kept["normed_t"], outs["normed_t"])
+
+    def project(at, cols, tile):
+        def step(k, carry):
+            here = pl.ds(pl.multiple_of(at + k * tile, 128), tile)
+            kept["lin"][:, here] = dot(normed[...], wbuf[:, here])
+            return carry
+
+        lax.fori_loop(0, cols // tile, step, 0)
+
+    def fetch(name, at, cols):
+        here = pl.ds(at, cols)
+        load(name, gp.at[:, here], wbuf.at[:, here])
+
+    advance(2)
+    advance(3)
+    advance(4)
+    fetch("qk", 0, 2 * KEYS)
+    advance(5)
+    fetch("v", 2 * KEYS, VALS)
+    loads["qk"].wait()
+    project(0, 2 * KEYS, 256)
+    advance(6)
+    fetch("gb", QKV, VALS + LANES)
+    loads["v"].wait()
+    project(2 * KEYS, VALS, 256)
+    loads["gb"].wait()
+    project(QKV, VALS, 256)
+    project(QKV + VALS, LANES, LANES)
+    store.put(kept["lin"], outs["lin"])
+    steps = mixer_forward(
+        rows, offsets, lengths, kept["lin"], kept["taps"], rate, bias, gain_o, kept["act"], kept["cum"],
+        kept["cum_t"], kept["tinv"], kept["fresh"], kept["heads"], mixed,
+    )
+    steps[0]()
+    steps[1]()
+    advance(7)
+    load("out", go, wobuf)
+    steps[2]()
+    advance(8)
+    steps[3]()
+    for name in ("act", "cum", "cum_t", "tinv", "fresh", "heads"):
+        store.put(kept[name], outs[name])
+    advance(9)
+    load("down", gd, wdbuf)
+    loads["out"].wait()
+
+    def out_step(k, carry):
+        here = pl.ds(pl.multiple_of(k * 256, 256), 256)
+        kept["middle"][:, here] = kept["xin"][:, here].astype(f32) + dot(mixed[...], wobuf[:, here])
+        return carry
+
+    lax.fori_loop(0, width // 256, out_step, 0)
+    store.put(kept["middle"], outs["middle"])
+    m = kept["middle"][...]
+    norm = m * lax.rsqrt(jnp.mean(m * m, axis=1, keepdims=True) + 1e-5) * gain2[...]
+    normed_mid[...] = norm.astype(bf16)
+    kept["normed_mid_t"][...] = transposed(norm)
+    store.put(kept["normed_mid_t"], outs["normed_mid_t"])
+    kept["mixed_t"][...] = transposed(mixed[...].astype(f32))
+    store.put(kept["mixed_t"], outs["mixed_t"])
+    advance(10)
+
+    def ffn(at, cols, up_at):
+        def step(k, carry):
+            here = pl.ds(pl.multiple_of(at + k * FTILE, FTILE), FTILE)
+            there = pl.ds(pl.multiple_of(ff + at + k * FTILE, FTILE), FTILE)
+            grad = dot(kept["dy"][...], wdbuf[here, :], 1, 1)
+            gate = dot(normed_mid[...], wbuf[:, here])
+            up = dot(normed_mid[...], wbuf[:, there])
+            sg = sigm(gate)
+            silu = gate * sg
+            hid = silu * up
+            kept["hidden"][:, here] = hid.astype(bf16)
+            kept["hidden_t"][here, :] = transposed(hid)
+            kept["grads_gu"][:, here] = (grad * up * (sg + silu * (1.0 - sg))).astype(bf16)
+            kept["grads_gu"][:, there] = (grad * silu).astype(bf16)
+            return carry
+
+        lax.fori_loop(0, cols // FTILE, step, 0)
+
+    low, high = pl.ds(0, FF_SPLIT), pl.ds(FF_SPLIT, ff - FF_SPLIT)
+    shift = lambda s: pl.ds(ff + s.start, s.size)
+    load("g0", gg.at[:, low], wbuf.at[:, low])
+    advance(11)
+    load("u0", gu.at[:, low], wbuf.at[:, shift(low)])
+    advance(12)
+    load("g1", gg.at[:, high], wbuf.at[:, high])
+    for name in ("down", "g0", "u0"):
+        loads[name].wait()
+    ffn(0, FF_SPLIT, 0)
+    advance(13)
+    load("u1", gu.at[:, high], wbuf.at[:, shift(high)])
+    loads["g1"].wait()
+    loads["u1"].wait()
+    ffn(FF_SPLIT, ff - FF_SPLIT, 0)
+    for name in ("hidden", "hidden_t", "grads_gu"):
+        store.put(kept[name], outs[name])
+    for c in first + exchange:
+        c.wait_send()
+    for f in made:
+        f.close()
+    store.wait()
+
+
+def forward_call(n_shard, reps, offs, lens, tokens, cot, deal, small_in, rate, bias, weights):
+    anywhere = pl.BlockSpec(memory_space=pl.ANY)
+    held = pl.BlockSpec(memory_space=pltpu.VMEM)
+    words = pl.BlockSpec(memory_space=pltpu.SMEM)
+    rows, width = tokens.shape
+    ff = weights[6].shape[1]
+    sd = jax.ShapeDtypeStruct
+    wide = QKV + VALS + LANES
+    vals_rows, ff_rows = weights[5].shape[0] * n_shard, weights[8].shape[0] * n_shard
+    gathered = [
+        sd((width, wide), bf16), sd((vals_rows, width), bf16), sd((width, ff), bf16), sd((width, ff), bf16),
+        sd((ff_rows, width), bf16),
+    ]
+    shapes = [fn(rows, width, ff) for _, fn in FORWARD_SAVED]
+    sems = pltpu.SemaphoreType.DMA
+    flows = 12
+    count = flows * Flow.COUNT(n_shard // 4)
+    scratch = [pltpu.VMEM(s, d) for s, d in shapes] + [
+        pltpu.VMEM((n_shard, 8, rows), jnp.int32), sems((n_shard,)), sems((n_shard,)),
+        pltpu.VMEM((n_shard, 16, width), bf16), sems((n_shard,)), sems((n_shard,)),
+        pltpu.VMEM((2, rows, width), bf16), pltpu.VMEM((2, rows, width), bf16), sems((2, n_shard)), sems((2, n_shard)),
+        pltpu.VMEM((width, 2 * ff), bf16), pltpu.VMEM((vals_rows, width), bf16), pltpu.VMEM((ff_rows, width), bf16),
+        sems((16,)), sems((count,)), sems((count,)), sems((flows,)), sems((len(shapes),)),
+        pltpu.VMEM((rows, width), bf16), pltpu.VMEM((rows, VALS), bf16), pltpu.VMEM((rows, width), bf16),
+    ]
+    res = pl.pallas_call(
+        functools.partial(forward_kernel, n_shard, reps),
+        in_specs=[words, words] + [held] * 6 + [anywhere] * 9,
+        out_specs=[anywhere] * (5 + len(shapes)),
+        out_shape=gathered + [sd(s, d) for s, d in shapes],
+        scratch_shapes=scratch,
+        compiler_params=pltpu.CompilerParams(collective_id=1, has_side_effects=True, vmem_limit_bytes=62 << 20),
+    )(offs, lens, tokens, cot, deal, small_in, rate, bias, *weights)
+    return res[:5], dict(zip([name for name, _ in FORWARD_SAVED], res[5:]))
+
+
+WIDE = 512
+NARROW = 256
+
+
+class Stream:
+    def __init__(self, buf, sem, parts):
+        self.buf, self.sem, self.parts, self.at = buf, sem, parts, 0
+        self.copies = {}
+
+    def start(self):
+        self.issue(0)
+
+    def issue(self, k):
+        if k < len(self.parts):
+            pairs = self.parts[k](self.buf.at[k % 2])
+            self.copies[k] = [pltpu.make_async_copy(s, d, self.sem.at[k % 2, i]) for i, (s, d) in enumerate(pairs)]
+            for c in self.copies[k]:
+                c.start()
+
+    def take(self):
+        k = self.at
+        self.at += 1
+        self.issue(k + 1)
+        for c in self.copies[k]:
+            c.wait()
+        return k, self.buf.at[k % 2]
+
+
+BACK_KEPT = tuple(name for name, _ in FORWARD_SAVED if name not in ("hidden",))
+
+
+def backward_kernel(n_shard, reps, rings, small, *refs):
+    take = iter(refs)
+    get = lambda k: [next(take) for _ in range(k)]
+    offs, lens, rate, bias = get(4)
+    gp, go, gg, gu, gd = get(5)
+    given = dict(zip(BACK_KEPT, get(len(BACK_KEPT))))
+    o_rows, o_grad, o_ffn, o_down, o_out, o_proj, o_small = get(7)
+    kept = dict(zip(BACK_KEPT, get(len(BACK_KEPT))))
     ring_a, ring_b = rings
-    load_sem = rest[0]
-    rest = rest[1:]
-    ring_a.bind(rest[:10])
-    ring_b.bind(rest[10:20])
-    small.bind(rest[20:23])
-    place = Place(n, reps)
+    ring_a.bind(get(10))
+    ring_b.bind(get(10))
+    small.bind(get(3))
+    (load_sem, wbuf, wsem, nbuf, nsem, acc, middle_grad, branch, mix_grad, dcols, drows, lin_grad, tap_grad, gain_grad,
+     rate_grad, bias_grad, small_v, sent, come, tsend, trecv, rows_out, out_sem) = get(23)
+    rows, width = kept["xin"].shape
+    ff = gg.shape[1]
+    per = rows // n_shard
+    place = Place(n_shard, reps)
+    p = place
+    offsets = [offs[i] for i in range(offs.shape[0])]
+    lengths = [lens[i] for i in range(lens.shape[0])]
+    loads = {}
+    order = (
+        "normed_mid_t", "grads_gu", "middle", "dy", "params", "hidden_t", "cum", "cum_t", "tinv", "fresh", "heads",
+        "act", "lin", "taps", "mixed_t", "normed_t", "xin", "pick", "place",
+    )
+    for k, name in enumerate(order):
+        loads[name] = pltpu.make_async_copy(given[name], kept[name], load_sem.at[k])
+        loads[name].start()
+    have = set()
+
+    def need(*names):
+        for name in names:
+            if name not in have:
+                have.add(name)
+                loads[name].wait()
+
     greet(place, True)
     pieces = []
-    loads = []
-    rows_a = gg.shape[3]
-
-    def add(ring, rows, cols, src, src_at, out, out_at):
-        piece = Piece(ring, place, rows, cols, out, out_at)
-        src_view = src.at[:, :, :, :, pl.ds(src_at, cols)]
-        pieces.append(piece)
-        loads.append(pltpu.make_async_copy(src_view, piece.own_view(), load_sem.at[len(pieces) % 2]))
-
-    for src, out in ((gg, og), (gu, ou)):
-        for at, width in FFN_CUTS:
-            add(ring_a, rows_a, width, src, at, out, at)
-    for at in range(0, 1024, 256):
-        add(ring_b, gd.shape[3], 256, gd, at, od, at)
-    for at in range(0, 1024, 256):
-        add(ring_b, go.shape[3], 256, go, at, oo, at)
-    at = 0
-    for out in (oq, ok, ov, ot, ob):
-        for inner, width in columns(out.shape[1], (768, 128)):
-            add(ring_a, rows_a, width, gp, at, out, inner)
-            at += width
-    value = small_in[...]
-    for index in range(len(pieces) + 7):
-        if index < 4:
-            small.begin(place, index, value)
+
+    def tick(piece=None, fill=None):
+        index = tick.index
+        tick.index += 1
         pump(pieces, index)
-        if index < len(pieces):
-            loads[index].start()
-            loads[index].wait()
-            pieces[index].send_core()
-        if index < 4:
-            value = small.end(index)
-    small_out[...] = value
-
-
-def scatter_sums(n, reps, gg, gu, gd, go, gp, small_in):
-    rings = (Ring(n, gg.shape[0] // n, 768), Ring(n, gd.shape[0] // n, 256))
-    small = Small(n, reps, *small_in.shape)
+        if piece is not None:
+            pieces.append(piece())
+            fill(pieces[-1])
+            pieces[-1].send_core()
+
+    tick.index = 0
+
+    def grad_piece(ring, size, left, right, cols, out, out_at):
+        def fill(piece):
+            def step(t, carry):
+                c, q = t % 2, t // 2
+                here = pl.ds(pl.multiple_of(t * size, 16), size)
+                value = dot(left[here, :], right)
+                ring.own[piece.slot, q // 2, q % 2, c, pl.ds(0, size), pl.ds(0, cols)] = value.astype(bf16)
+                return carry
+
+            lax.fori_loop(0, n_shard, step, 0)
+
+        tick(lambda: Piece(ring, place, size, cols, out, out_at), fill)
+
+    rows_a = width // n_shard
+
+    def gu_piece(k):
+        need("normed_mid_t", "grads_gu")
+        at = k * WIDE
+        grad_piece(ring_a, rows_a, kept["normed_mid_t"], kept["grads_gu"][:, at : at + WIDE], WIDE, o_ffn, at)
+
+    def down_piece(k):
+        need("hidden_t", "dy")
+        at = k * NARROW
+        grad_piece(ring_b, ff // n_shard, kept["hidden_t"], kept["dy"][:, at : at + NARROW], NARROW, o_down, at)
+
+    def out_piece(k):
+        need("mixed_t")
+        at = k * NARROW
+        grad_piece(ring_b, VALS // n_shard, kept["mixed_t"], branch[:, at : at + NARROW], NARROW, o_out, at)
+
+    def proj_piece(at, cols):
+        need("normed_t")
+        grad_piece(ring_a, rows_a, kept["normed_t"], lin_grad[:, at : at + cols], cols, o_proj, at)
+
+    def gu_part(k):
+        cols = pl.ds(k * FTILE, FTILE)
+        return lambda b: [(gg.at[:, cols], b.at[:, pl.ds(0, FTILE)]), (gu.at[:, cols], b.at[:, pl.ds(FTILE, FTILE)])]
+
+    chunks = ff // FTILE
+    gu_stream = Stream(wbuf, wsem, [gu_part(k) for k in range(chunks)])
+
+    def gnm(count):
+        need("grads_gu")
+        for _ in range(count):
+            k, buf = gu_stream.take()
+            at = k * FTILE
+            part = dot(kept["grads_gu"][:, at : at + FTILE], buf[:, 0:FTILE], 1, 1)
+            part = part + dot(kept["grads_gu"][:, ff + at : ff + at + FTILE], buf[:, FTILE : 2 * FTILE], 1, 1)
+            acc[...] = part if k == 0 else acc[...] + part
+
+    def norm_back(values, gain, upstream):
+        n = lax.rsqrt(jnp.mean(values * values, axis=1, keepdims=True) + 1e-5)
+        u = upstream * gain
+        gain_part = jnp.sum(upstream * values * n, axis=0, keepdims=True)
+        return n * (u - values * (n * n) * jnp.mean(u * values, axis=1, keepdims=True)), gain_part
+
+    def norm2():
+        need("middle", "dy", "params")
+        back, gain_part = norm_back(kept["middle"][...], kept["params"][13:14, :], acc[...])
+        small_v[13:14, :] = gain_part
+        total = kept["dy"][...].astype(f32) + back
+        middle_grad[...] = total
+        branch[...] = total.astype(bf16)
+
+    def row_part(src, k):
+        return lambda b: [(src.at[pl.ds(k * FTILE, FTILE), :], b)]
+
+    out_stream = Stream(nbuf, nsem, [row_part(go, k) for k in range(VALS // FTILE)])
+    down_stream = Stream(nbuf, nsem, [row_part(gd, k) for k in range(chunks)])
+
+    def grad_mixed(count):
+        for _ in range(count):
+            k, buf = out_stream.take()
+            mix_grad[:, k * FTILE : (k + 1) * FTILE] = dot(branch[...], buf[...], 1, 1)
+
+    def result(count):
+        need("hidden_t", "middle")
+        for _ in range(count):
+            k, buf = down_stream.take()
+            part = dot(kept["hidden_t"][k * FTILE : (k + 1) * FTILE, :], buf[...], 0, 0)
+            acc[...] = (kept["middle"][...] if k == 0 else acc[...]) + part
+
+    exchange = {}
+
+    def send_home(a, value):
+        need("place")
+        here = pl.ds(pl.multiple_of(p.s * per, 16), per)
+        for at in range(0, width, 256):
+            sent[a, :, at : at + 256] = dot(kept["place"][...], value[:, at : at + 256]).astype(bf16)
+        exchange[a] = []
+        for d in range(1, n_shard):
+            t = (p.s + d) % n_shard
+            exchange[a].append(
+                remote(
+                    sent.at[a, pl.ds(pl.multiple_of(t * per, 16), per)], come.at[a, here],
+                    tsend.at[a, d], trecv.at[a, d], (p.r, t),
+                )
+            )
+            exchange[a][-1].start()
+        come[a, here, :] = sent[a, here, :]
+
+    stores = []
+
+    def arrive(a, out):
+        need("pick")
+        for c in exchange[a]:
+            c.wait()
+        for at in range(0, width, 256):
+            rows_out[a, :, at : at + 256] = dot(kept["pick"][...], come[a, :, at : at + 256], 0, 0).astype(bf16)
+        stores.append(pltpu.make_async_copy(rows_out.at[a], out, out_sem.at[a]))
+        stores[-1].start()
+
+    def wide_part(at, cols):
+        return lambda b: [(gp.at[:, pl.ds(at, cols)], b.at[:, pl.ds(0, cols)])]
+
+    proj_cuts = [(at, WIDE) for at in range(0, QKV + VALS, WIDE)] + [(QKV + VALS, LANES)]
+    proj_stream = Stream(wbuf, wsem, [wide_part(at, cols) for at, cols in proj_cuts])
+
+    def grad_normed(count):
+        for _ in range(count):
+            k, buf = proj_stream.take()
+            at, cols = proj_cuts[k]
+            part = dot(lin_grad[:, at : at + cols], buf[:, 0:cols], 1, 1)
+            acc[...] = part if k == 0 else acc[...] + part
+
+    def norm1():
+        need("xin")
+        back, gain_part = norm_back(kept["xin"][...].astype(f32), kept["params"][12:13, :], acc[...])
+        small_v[12:13, :] = gain_part
+        rows_out[1] = (middle_grad[...] + back).astype(bf16)
+
+    def pack_small():
+        small_v[14:16, :] = jnp.zeros((2, width), f32)
+        for t in range(4):
+            for g in range(QKV // width):
+                row = t * (QKV // width) + g
+                small_v[row : row + 1, :] = tap_grad[t : t + 1, g * width : (g + 1) * width]
+        small_v[14:15, 0:DVH] = gain_grad[...]
+        small_v[14:15, DVH : DVH + LANES] = rate_grad[...]
+        small_v[14:15, DVH + LANES : DVH + 2 * LANES] = bias_grad[...]
+
+    gu_stream.start()
+    gu_piece(0)
+    gnm(2)
+    gu_piece(1)
+    gnm(3)
+    gu_piece(2)
+    gnm(3)
+    gu_piece(3)
+    gnm(3)
+    out_stream.start()
+    gu_piece(4)
+    norm2()
+    gu_piece(5)
+    grad_mixed(VALS // FTILE)
+    need("cum", "cum_t", "tinv", "fresh", "heads", "act", "lin", "taps")
+    clear, heads, rates, convs = mixer_backward(
+        rows, offsets, lengths, kept["lin"], kept["taps"], rate, bias, kept["params"].at[14:15, 0:DVH], kept["act"],
+        kept["cum"], kept["cum_t"], kept["tinv"], kept["fresh"], kept["heads"], mix_grad,
+        kept["act"], dcols, drows, lin_grad, tap_grad, gain_grad, rate_grad, bias_grad,
+    )
+    clear()
+    gu_piece(6)
+    heads[0]()
+    gu_piece(7)
+    heads[1]()
+    gu_piece(8)
+    heads[2]()
+    gu_piece(9)
+    heads[3]()
+    gu_piece(10)
+    heads[4]()
+    down_piece(0)
+    heads[5]()
+    down_piece(1)
+    rates()
+    convs[0]()
+    down_piece(2)
+    down_stream.start()
+    convs[1]()
+    down_piece(3)
+    result(chunks // 2)
+    out_piece(0)
+    result(chunks - chunks // 2)
+    rows_out[0] = acc[...].astype(bf16)
+    send_home(0, rows_out.at[0])
+    proj_stream.start()
+    out_piece(1)
+    grad_normed(5)
+    out_piece(2)
+    grad_normed(len(proj_cuts) - 5)
+    out_piece(3)
+    norm1()
+    send_home(1, rows_out.at[1])
+    pack_small()
+    value = small_v[...]
+    for k, (at, cols) in enumerate(proj_cuts[6:9] + proj_cuts[0:6] + proj_cuts[9:]):
+        if 1 <= k <= 4:
+            small.begin(place, k - 1, value)
+        proj_piece(at, cols)
+        if 1 <= k <= 4:
+            value = small.end(k - 1)
+        if k == 5:
+            arrive(0, o_rows)
+        if k == 7:
+            arrive(1, o_grad)
+    for _ in range(7):
+        tick()
+    o_small[...] = value
+    for c in stores:
+        c.wait()
+
+
+def backward_call(n_shard, reps, offs, lens, rate, bias, gathered, saved):
     anywhere = pl.BlockSpec(memory_space=pl.ANY)
     held = pl.BlockSpec(memory_space=pltpu.VMEM)
-    rows = gg.shape[0] // n
-
-    def shards(g):
-        return g.reshape(n // 4, 2, 2, g.shape[0] // n, g.shape[1])
-
-    shape = lambda r, c: jax.ShapeDtypeStruct((r, c), bf16)
+    words = pl.BlockSpec(memory_space=pltpu.SMEM)
+    rows, width = saved["xin"].shape
+    ff = gathered[2].shape[1]
+    sd = jax.ShapeDtypeStruct
+    wide = QKV + VALS + LANES
+    sems = pltpu.SemaphoreType.DMA
+    rings = (Ring(n_shard, width // n_shard, WIDE), Ring(n_shard, ff // n_shard, NARROW))
+    small = Small(n_shard, reps, 16, width)
     outs = [
-        shape(rows, gg.shape[1]), shape(rows, gu.shape[1]), shape(gd.shape[0] // n, gd.shape[1]),
-        shape(go.shape[0] // n, go.shape[1]), shape(rows, KEYS), shape(rows, KEYS), shape(rows, VALS),
-        shape(rows, VALS), shape(rows, LANES), jax.ShapeDtypeStruct(small_in.shape, f32),
+        sd((rows, width), bf16), sd((rows, width), bf16), sd((width // n_shard, 2 * ff), bf16),
+        sd((ff // n_shard, width), bf16), sd((VALS // n_shard, width), bf16), sd((width // n_shard, wide), bf16),
+        sd((16, width), f32),
+    ]
+    vmem = pltpu.VMEM
+    scratch = [vmem(saved[name].shape, saved[name].dtype) for name in BACK_KEPT]
+    scratch += rings[0].scratch() + rings[1].scratch() + small.scratch()
+    scratch += [
+        sems((len(BACK_KEPT),)), vmem((2, width, WIDE), bf16), sems((2, 2)), vmem((2, FTILE, width), bf16), sems((2, 1)),
+        vmem((rows, width), f32), vmem((rows, width), f32), vmem((rows, width), bf16), vmem((rows, VALS), f32),
+        vmem((rows, LANES), f32), vmem((LANES, rows), f32), vmem((rows, wide), bf16), vmem((4, QKV), f32),
+        vmem((1, DVH), f32), vmem((1, LANES), f32), vmem((1, LANES), f32), vmem((16, width), f32),
+        vmem((2, rows, width), bf16), vmem((2, rows, width), bf16), sems((2, n_shard)), sems((2, n_shard)),
+        vmem((2, rows, width), bf16), sems((2,)),
     ]
     return pl.pallas_call(
-        functools.partial(scatter_kernel, n, reps, rings, small),
+        functools.partial(backward_kernel, n_shard, reps, rings, small),
+        in_specs=[words, words, held, held] + [anywhere] * (5 + len(BACK_KEPT)),
+        out_specs=[anywhere] * 6 + [held],
         out_shape=outs,
-        in_specs=[anywhere] * 5 + [held],
-        out_specs=[anywhere] * 9 + [held],
-        scratch_shapes=[pltpu.SemaphoreType.DMA((2,))] + rings[0].scratch() + rings[1].scratch() + small.scratch(),
-        compiler_params=pltpu.CompilerParams(collective_id=0, has_side_effects=True, vmem_limit_bytes=60 << 20),
-    )(shards(gg), shards(gu), shards(gd), shards(go), shards(gp), small_in)
-
-
-def forward_call(n, offs, lens, lin, taps, rate, bias, gain):
-    held = pl.BlockSpec(memory_space=pltpu.VMEM)
-    words = pl.BlockSpec(memory_space=pltpu.SMEM)
-
-    def kernel(offs, lens, *refs):
-        count = offs.shape[0]
-        mixer_forward(n, [offs[i] for i in range(count)], [lens[i] for i in range(count)], *refs)
-
-    sd = lambda s, d=f32: jax.ShapeDtypeStruct(s, d)
-    return pl.pallas_call(
-        kernel,
-        in_specs=[words, words] + [held] * 5,
-        out_specs=[held] * 7,
-        out_shape=[sd((n, QKV)), sd((n, LANES)), sd((LANES, n)), sd((HEADS, n, n)), sd((n, VALS)), sd((n, VALS)), sd((n, VALS), bf16)],
-        compiler_params=pltpu.CompilerParams(vmem_limit_bytes=56 << 20),
-    )(offs, lens, lin, taps, rate, bias, gain)
-
-
-def backward_call(n, offs, lens, lin, taps, rate, bias, gain, saved, grad_mixed):
-    held = pl.BlockSpec(memory_space=pltpu.VMEM)
-    words = pl.BlockSpec(memory_space=pltpu.SMEM)
-
-    def kernel(offs, lens, *refs):
-        count = offs.shape[0]
-        mixer_backward(n, [offs[i] for i in range(count)], [lens[i] for i in range(count)], *refs)
-
-    sd = lambda s, d=f32: jax.ShapeDtypeStruct(s, d)
-    wide = QKV + VALS + LANES
-    return pl.pallas_call(
-        kernel,
-        in_specs=[words, words] + [held] * 12,
-        out_specs=[held] * 8,
-        out_shape=[sd((n, QKV)), sd((n, LANES)), sd((LANES, n)), sd((n, wide), bf16), sd((4, QKV)), sd((1, DVH)), sd((1, LANES)), sd((1, LANES))],
-        compiler_params=pltpu.CompilerParams(vmem_limit_bytes=56 << 20),
-    )(offs, lens, lin, taps, rate, bias, gain, *saved, grad_mixed)
-
-
-def mm(a, b):
-    return jnp.dot(a, b, preferred_element_type=f32)
+        scratch_shapes=scratch,
+        compiler_params=pltpu.CompilerParams(collective_id=0, has_side_effects=True, vmem_limit_bytes=63 << 20),
+    )(offs, lens, rate, bias, *gathered, *[saved[name] for name in BACK_KEPT])
 
 
 def local(
@@ -703,85 +1302,43 @@
 ):
     rows, width = tokens.shape
     n = lax.axis_size("shard")
-    per_peer = rows // n
-    source = deal // rows
-    local_row = deal % rows
-    slot_order = jnp.argsort(source, stable=True)
-    wanted = local_row[slot_order].reshape(n, per_peer)
-    swap = functools.partial(lax.all_to_all, axis_name="shard", split_axis=0, concat_axis=0, tiled=True)
-    asked = swap(wanted).reshape(rows)
-    slot_place = jnp.argsort(slot_order)
-    block_in = swap(tokens[asked].reshape(n, per_peer, width)).reshape(rows, width)[slot_place]
-    block_dy = swap(cotangent[asked].reshape(n, per_peer, width)).reshape(rows, width)[slot_place]
-    given_place = jnp.argsort(asked)
-    gather = functools.partial(lax.all_gather, axis_name="shard", axis=0, tiled=True)
+    s = lax.axis_index("shard")
     pad = LANES - 2 * HEADS
     bd_weight = jnp.concatenate([beta_weight, decay_weight, jnp.zeros((beta_weight.shape[0], pad), bf16)], axis=1)
-    proj = [gather(w) for w in (q_weight, k_weight, v_weight, out_gate_weight, bd_weight)]
-    gain1, gain2, gain_o = [gather(g).astype(f32)[None, :] for g in (norm1_gain, norm2_gain, out_norm_gain)]
-    taps = lax.all_gather(conv_weight, "shard", axis=1, tiled=True).astype(f32)
-    w_out, w_gate, w_up, w_down = [gather(w) for w in (out_weight, ffn_gate, ffn_up, ffn_down)]
     lanes = lambda a: jnp.pad(a, (HEADS, LANES - 2 * HEADS))[None, :]
     rate, bias = lanes(log_rate), lanes(step_bias)
 
-    x = block_in.astype(f32)
-    r1 = lax.rsqrt(jnp.mean(x * x, axis=-1, keepdims=True) + 1e-5)
-    normed_in = (x * r1 * gain1).astype(bf16)
-    lin = jnp.concatenate([mm(normed_in, w) for w in proj], axis=1)
-    saved = forward_call(rows, offsets[0], lengths[0], lin, taps, rate, bias, gain_o)
-    mixed = saved[6]
-    middle = x + mm(mixed, w_out)
-    r2 = lax.rsqrt(jnp.mean(middle * middle, axis=-1, keepdims=True) + 1e-5)
-    normed_mid = (middle * r2 * gain2).astype(bf16)
-    gate, up = mm(normed_mid, w_gate), mm(normed_mid, w_up)
-    sg = jax.nn.sigmoid(gate)
-    hidden = (gate * sg * up).astype(bf16)
-    result = (middle + mm(hidden, w_down)).astype(bf16)
-    grad_down = mm(hidden.T, block_dy).astype(bf16)
-    grad_hidden = mm(block_dy, w_down.T)
-    grad_gate = (grad_hidden * up * (sg + gate * sg * (1.0 - sg))).astype(bf16)
-    grad_up = (grad_hidden * gate * sg).astype(bf16)
-    g_gate = mm(normed_mid.T, grad_gate).astype(bf16)
-    g_up = mm(normed_mid.T, grad_up).astype(bf16)
-    gnm = mm(grad_gate, w_gate.T) + mm(grad_up, w_up.T)
-    g_norm2 = jnp.sum(gnm * middle * r2, axis=0)
-    u = gnm * gain2
-    grad_middle = block_dy.astype(f32) + r2 * (u - middle * (r2 * r2) * jnp.mean(u * middle, axis=-1, keepdims=True))
-    branch = grad_middle.astype(bf16)
-    g_out = mm(mixed.T, branch).astype(bf16)
-    grad_mixed = mm(branch, w_out.T)
-    back = backward_call(rows, offsets[0], lengths[0], lin, taps, rate, bias, gain_o, saved[:6], grad_mixed)
-    lin_grad = back[3]
-    g_proj = mm(normed_in.T, lin_grad).astype(bf16)
-    grad_normed = mm(lin_grad, jnp.concatenate(proj, axis=1).T)
-    g_norm1 = jnp.sum(grad_normed * x * r1, axis=0)
-    u = grad_normed * gain1
-    grad_in = (grad_middle + r1 * (u - x * (r1 * r1) * jnp.mean(u * x, axis=-1, keepdims=True))).astype(bf16)
-
-    flat = jnp.concatenate([back[5][0], back[6][0], back[7][0]])
-    small = jnp.concatenate(
-        [
-            back[4].reshape(-1, width), g_norm1[None], g_norm2[None],
-            jnp.pad(flat, (0, width - flat.shape[0]))[None], jnp.zeros((1, width), f32),
-        ],
-        axis=0,
+    def spread(vector):
+        size = vector.shape[0]
+        wide = lax.dynamic_update_slice(jnp.zeros((size * n,), bf16), vector, (s * size,))
+        return jnp.pad(wide, (0, width - size * n))[None]
+
+    taps = lax.dynamic_update_slice(jnp.zeros((4, QKV), bf16), conv_weight, (0, s * conv_weight.shape[1]))
+    small_in = jnp.concatenate(
+        [taps.reshape(-1, width), spread(norm1_gain), spread(norm2_gain), spread(out_norm_gain), jnp.zeros((1, width), bf16)]
     )
-    sums = scatter_sums(n, reps, g_gate, g_up, grad_down, g_out, g_proj, small)
-    small = sums[9]
-    s = lax.axis_index("shard")
+    weights = (q_weight, k_weight, v_weight, out_gate_weight, bd_weight, out_weight, ffn_gate, ffn_up, ffn_down)
+    deals = jnp.broadcast_to(deal[None, :], (8, rows))
+    gathered, saved = forward_call(
+        n, reps, offsets[0], lengths[0], tokens, cotangent, deals, small_in, rate, bias, weights
+    )
+    home_rows, home_grad, s_ffn, s_down, s_out, s_proj, small = backward_call(
+        n, reps, offsets[0], lengths[0], rate, bias, gathered, saved
+    )
 
     def part(a, dim=0):
         size = a.shape[dim] // n
         return lax.dynamic_slice_in_dim(a, s * size, size, dim)
 
-    home = lambda a: swap(a[slot_order].reshape(n, per_peer, width)).reshape(rows, width)[given_place]
     f = lambda a: a.astype(f32)
-    bd = sums[8]
+    ff = ffn_gate.shape[1]
+    at = QKV + VALS
     return (
-        home(result), home(grad_in), part(small[12]), f(sums[4]), f(sums[5]), f(sums[6]),
-        part(small[:12].reshape(4, QKV), 1), f(bd[:, :HEADS]), f(bd[:, HEADS : 2 * HEADS]),
-        small[14, DVH + HEADS : DVH + 2 * HEADS], small[14, DVH + LANES + HEADS : DVH + LANES + 2 * HEADS],
-        f(sums[7]), part(small[14, :DVH]), f(sums[3]), part(small[13]), f(sums[0]), f(sums[1]), f(sums[2]),
+        home_rows, home_grad, part(small[12]), f(s_proj[:, :KEYS]), f(s_proj[:, KEYS : 2 * KEYS]),
+        f(s_proj[:, 2 * KEYS : QKV]), part(small[:12].reshape(4, QKV), 1), f(s_proj[:, at : at + HEADS]),
+        f(s_proj[:, at + HEADS : at + 2 * HEADS]), small[14, DVH + HEADS : DVH + 2 * HEADS],
+        small[14, DVH + LANES + HEADS : DVH + LANES + 2 * HEADS], f(s_proj[:, QKV:at]), part(small[14, :DVH]),
+        f(s_out), part(small[13]), f(s_ffn[:, :ff]), f(s_ffn[:, ff:]), f(s_down),
     )
 
 

time: 618 us -> 395 us (0.64)
  waiting for transfers between devices: 133 us -> 0 us
  Pallas kernels: 242 us -> 362 us
  matrix products: 77.8 us -> 0 us
  blocking collectives: 62.9 us -> 0 us
  local copies, waits for them, and re-layouts: 39.6 us -> 19.4 us
  between operations: 15.8 us -> 0.95 us
  starting transfers between devices: 14.5 us -> 0 us
  other arithmetic: 22.7 us -> 8.84 us
    all_gather x8 -> x0, waiting for transfers between devices: 125 us -> none  [local(): gather(w)]
    pallas_call x3 -> x2, Pallas kernels: 242 us -> 362 us  [the longest x1 193 us: backward_call(): pl.pallas_call(functools.partial(backward_kernel, n_shard, reps, rings, s...]
    dot_general x19 -> x0, matrix products: 77.8 us -> none  [mm(): return jnp.dot(a, b, preferred_element_type=f32)]
    all_gather x4 -> x0, blocking collectives: 39.9 us -> none  [the longest x2 15.4 us: local(): gather(g).astype(f32)[None, :]]
    gather x9 -> x0, local copies, waits for them, and re-layouts: 16 us -> none  [the longest x2 3.92 us: local(): a[slot_order].reshape(n, per_peer, width)]
    all_to_all x4 -> x0, starting transfers between devices: 14.2 us -> none  [the longest x2 7.25 us: local(): swap(a[slot_order].reshape(n, per_peer, width)).reshape(rows, width)]
    unnamed x1 -> x0, blocking collectives: 13.3 us -> none
    all_to_all x1 -> x0, blocking collectives: 9.75 us -> none  [local(): asked = swap(wanted).reshape(rows)]
  transfers between devices with their start and end apart: 12 -> 0, of which waited for: 5 -> 0; matrix products, arithmetic and copies ran while one was open for 14% -> 0% of each run, Pallas kernels for 35% -> 0%
where the time goes in v2:
time: 395 us; the launch traced here: 391 us
  Pallas kernels  362 us (92%)
  local copies, waits for them, and re-layouts  19.4 us (5%)
  other arithmetic  8.84 us (2%)
    pallas_call x1, Pallas kernels, backward_call(): pl.pallas_call(functools.partial(backward_kernel, n_shard, reps, rings, s...  193 us
    pallas_call x1, Pallas kernels, forward_call(): pl.pallas_call(functools.partial(forward_kernel, n_shard, reps), in_specs...  169 us
    convert_element_type x6, other arithmetic, local(): f = lambda a: a.astype(f32)  8.14 us

profile of v2, /device:TPU:0, one launch (start us, length us, event | category | flops | bytes accessed | tf_op | source)
XLA Modules:
  0.0 390.8 jit_solution(2753021332118416375)
XLA Ops:
  0.7 1.2 pad_bitcast_fusion.1.refs_6_.refs_2_
  1.9 1.2 pad_bitcast_fusion.refs_7_.refs_3_
  3.2 0.8 dynamic_update_slice.17
  4.1 0.7 constant_dynamic-update-slice_fusion
  5.4 1.3 broadcast_in_dim.35.refs_4_
  6.7 0.7 constant_dynamic-update-slice_fusion.2
  7.5 2.0 concatenate.6.refs_5_
  9.4 0.8 copy.39
  10.2 0.8 copy.40
  11.1 0.7 maximum_maximum_fusion.refs_12_
  11.8 168.8 %shard_map.340 = (bf16[1024,4736]{1,0:T(8,128)(2,1)}, bf16[1536,1024]{1,0:T(8,128)(2,1)}, bf16[1024,2816]{1,0:T(8,128)(2,1)}, bf16[1024,2816]{1,0:T(8,128)(2,1)}...) custom-call(s32[4]{0:T(128)} %bitcast.22, ...), custom_call_target="tpu_custom_call" | custom-call | tf_op jit(solution)/shard_map/pallas_call | solution.py:955
  180.5 192.8 %shard_map.341 = (bf16[256,1024]{1,0:T(8,128)(2,1)}, bf16[256,1024]{1,0:T(8,128)(2,1)}, bf16[128,5632]{1,0:T(8,128)(2,1)}, bf16[352,1024]{1,0:T(8,128)(2,1)}, bf...) custom-call(s32[4]{0:T(128)} %bitcast.23, s32[4]{0:T(128)} %bitcast.25, ...), custom_call_target="tpu_custom_call" | custom-call | tf_op jit(solution)/shard_map/pallas_call | solution.py:1288
  373.4 0.8 slice.52
  374.7 1.3 slice_bitcast_fusion
  376.0 0.8 fusion.3
  377.4 0.9 reshape.51
  378.8 0.9 slice_convert_fusion.6
  381.1 2.0 convert_element_type.41
  383.0 0.9 slice_convert_fusion.4
  384.0 1.3 slice_convert_fusion.2
  385.3 1.3 convert_element_type.44
  387.2 1.8 slice_convert_fusion
  389.0 0.8 copy.50
  389.7 0.8 copy.51
  (26 shorter events, 4.5 us)
Async XLA Ops:
  373.3 9.7 %copy-start.1 = (bf16[128,4736]{1,0:T(8,128)(2,1)S(1)}, bf16[128,4736]{1,0:T(8,128)(2,1)}, u32[]{:S(2)}) copy-start(bf16[128,4736]{1,0:T(8,128)(2,1)} %get-tuple-element.76) | copy-start | bytes 3637252
  384.0 1.3 copy-start.2
  385.3 1.9 copy-start
  387.2 1.8 copy-start.4
  387.2 2.6 copy-start.3

commit v3 on v2

--- a/solution.py
+++ b/solution.py
@@ -132,14 +132,7 @@
         scaled = o * lax.rsqrt(jnp.mean(o * o, axis=1, keepdims=True) + 1e-5)
         mixed[:, vcols] = (scaled * gain[...] * (gate * sigm(gate))).astype(bf16)
 
-    def pair(step):
-        def run():
-            one_head(2 * step)
-            one_head(2 * step + 1)
-
-        return run
-
-    return [convolve] + [pair(step) for step in range(HEADS // 2)]
+    return convolve, [functools.partial(one_head, h) for h in range(HEADS)]
 
 
 def mixer_backward(
@@ -516,13 +509,13 @@
 
 def pump(pieces, index):
     stages = [
+        (1, lambda q: q.after_core()),
         (7, lambda q: q.close()),
         (6, lambda q: q.finish(False)),
         (5, lambda q: q.finish(True)),
         (4, lambda q: q.after_up()),
         (3, lambda q: q.after_second()),
         (2, lambda q: q.after_first()),
-        (1, lambda q: q.after_core()),
     ]
     for lag, act in stages:
         if 0 <= index - lag < len(pieces):
@@ -574,25 +567,35 @@
 
 
 class Flow:
-    COUNT = staticmethod(lambda ys: 3 + 6 * (ys - 1))
-
-    def __init__(self, place, src, src_at, cols, dst, dst_at, send, recv, base, mine):
-        self.p, self.rows = place, src.shape[0]
-        self.src = src.at[:, pl.ds(src_at, cols)]
-        self.dst, self.cols = dst, pl.ds(dst_at, cols)
+    @staticmethod
+    def count(ys, pair):
+        return 5 + 12 * (ys - 1) if pair else 3 + 6 * (ys - 1)
+
+    def __init__(self, place, src, src_at, cols, dst, dst_at, pair, send, recv, base, mine):
+        self.p, self.rows, self.pair = place, src.shape[0], pair
+        self.src_ref, self.src_at, self.dst, self.dst_at, self.width = src, src_at, dst, dst_at, cols
         self.send, self.recv, self.base, self.used = send, recv, base, 0
         self.ra = halved(self.rows)
-        self.mine = pltpu.make_async_copy(self.src, self.region(place.y, place.x, place.c), mine)
+        self.part = (place.r % 2) if pair else None
+        whole = self.src_ref.at[:, pl.ds(src_at, cols)]
+        self.mine = pltpu.make_async_copy(whole, self.region(place.y, place.x, place.c), mine)
+        self.whole = whole
         self.all = []
 
-    def region(self, y, x, c, half=None):
+    def columns(self, at, part):
+        if part is None:
+            return pl.ds(at, self.width)
+        half = self.width // 2
+        return pl.ds(pl.multiple_of(at + part * half, LANES), half)
+
+    def region(self, y, x, c, half=None, part=None):
         start = ((y * 2 + x) * 2 + c) * self.rows
         size = self.rows
         if half == 0:
             size = self.ra
         elif half == 1:
             start, size = start + self.ra, self.rows - self.ra
-        return self.dst.at[pl.ds(pl.multiple_of(start, 16), size), self.cols]
+        return self.dst.at[pl.ds(pl.multiple_of(start, 16), size), self.columns(self.dst_at, part)]
 
     def copy(self, dst, device, src=None):
         at = self.base + self.used
@@ -604,31 +607,44 @@
 
     def begin(self):
         p = self.p
-        own = self.region(p.y, p.x, p.c)
+        own = self.region(p.y, p.x, p.c, None, self.part)
+        src = self.src_ref.at[:, self.columns(self.src_at, self.part)]
         self.mine.start()
-        self.from_x = self.copy(own, p.x_peer(), self.src)
-        self.from_y = [self.copy(own, p.y_peer(d), self.src) for d in range(1, p.ys)]
-        self.from_core = [self.copy(own, p.core_peer(), self.src)]
+        self.from_x = self.copy(own, p.x_peer(), src)
+        self.from_y = [self.copy(own, p.y_peer(d), src) for d in range(1, p.ys)]
+        self.from_core = [self.copy(self.region(p.y, p.x, p.c), p.core_peer(), self.whole)]
+        self.from_z, self.z_regions = [], []
+
+    def share(self, *where):
+        p = self.p
+        if self.pair:
+            self.from_z.append(self.copy(self.region(*where, self.part), (p.r + 1 - 2 * (p.r % 2), p.s)))
+            self.z_regions.append(where)
+        self.from_core.append(self.copy(self.region(*where, self.part), p.core_peer()))
 
     def forward(self):
         p = self.p
         steps = range(1, p.ys)
         self.from_x.wait_recv()
-        self.diag = [self.copy(self.region(p.y, 1 - p.x, p.c, 0), p.y_peer(d)) for d in steps]
-        self.from_core.append(self.copy(self.region(p.y, 1 - p.x, p.c), p.core_peer()))
+        self.diag = [self.copy(self.region(p.y, 1 - p.x, p.c, 0, self.part), p.y_peer(d)) for d in steps]
+        self.share(p.y, 1 - p.x, p.c, None)
         for d in steps:
             self.from_y[d - 1].wait_recv()
             back = p.y_of(p.ys - d)
-            self.diag.append(self.copy(self.region(back, p.x, p.c, 1), p.x_peer()))
-            self.from_core.append(self.copy(self.region(back, p.x, p.c), p.core_peer()))
+            self.diag.append(self.copy(self.region(back, p.x, p.c, 1, self.part), p.x_peer()))
+            self.share(back, p.x, p.c, None)
 
     def relay(self):
         p = self.p
         for i, c in enumerate(self.diag):
             c.wait_recv()
             half, d = divmod(i, p.ys - 1)
-            back = p.y_of(p.ys - d - 1)
-            self.from_core.append(self.copy(self.region(back, 1 - p.x, p.c, half), p.core_peer()))
+            self.share(p.y_of(p.ys - d - 1), 1 - p.x, p.c, half)
+
+    def swap(self):
+        for c, where in zip(self.from_z, self.z_regions):
+            c.wait_recv()
+            self.from_core.append(self.copy(self.region(*where, 1 - self.part), self.p.core_peer()))
 
     def done(self):
         for c in self.from_core:
@@ -700,11 +716,17 @@
     kept = dict(zip([name for name, _ in FORWARD_SAVED], get(len(FORWARD_SAVED))))
     (dealt, dsend, drecv, smalls, ssend, srecv, sent, come, tsend, trecv, wbuf, wobuf, wdbuf, load_sem, fsend, frecv,
      mine_sem, out_sem, normed, mixed, normed_mid) = get(21)
+    shards, shard_sem = get(9), get(1)[0]
+    own_loads = []
+    for k, (w, v) in enumerate(zip((wq, wk, wv, wt, wb, wo, wd, wg, wu), shards)):
+        own_loads.append(pltpu.make_async_copy(w, v, shard_sem.at[k]))
+        own_loads[-1].start()
+    wq, wk, wv, wt, wb, wo, wd, wg, wu = shards
     rows, width = tokens.shape
     per = rows // n_shard
     place = Place(n_shard, reps)
     p = place
-    greet(place, False)
+    greet(place, True)
     offsets = [offs[i] for i in range(offs.shape[0])]
     lengths = [lens[i] for i in range(lens.shape[0])]
     store = Store(out_sem)
@@ -721,33 +743,50 @@
         first.append(remote(smalls.at[p.s], smalls.at[p.s], ssend.at[d], srecv.at[d], to))
         first[-1].start()
 
-    per_flow = Flow.COUNT(p.ys)
     made = []
 
-    def flow(src, at, cols, dst, dst_at):
+    def flow(src, at, cols, dst, dst_at, pair):
         k = len(made)
-        made.append(Flow(place, src, at, cols, dst, dst_at, fsend, frecv, k * per_flow, mine_sem.at[k]))
+        base = sum(Flow.count(p.ys, f.pair) for f in made)
+        made.append(Flow(place, src, at, cols, dst, dst_at, pair, fsend, frecv, base, mine_sem.at[k]))
         return made[-1]
 
     ff = wg.shape[1]
     stages = [
-        [flow(wq, 0, KEYS, gp, 0), flow(wk, 0, KEYS, gp, KEYS)],
-        [flow(wv, 0, VALS, gp, 2 * KEYS)],
-        [flow(wt, 0, VALS, gp, QKV), flow(wb, 0, LANES, gp, QKV + VALS)],
-        [flow(wo, 0, width, go, 0)],
-        [flow(wd, 0, width // 2, gd, 0)],
-        [flow(wd, width // 2, width // 2, gd, width // 2)],
-        [flow(wg, 0, FF_SPLIT, gg, 0)],
-        [flow(wu, 0, FF_SPLIT, gu, 0)],
-        [flow(wg, FF_SPLIT, ff - FF_SPLIT, gg, FF_SPLIT)],
-        [flow(wu, FF_SPLIT, ff - FF_SPLIT, gu, FF_SPLIT)],
+        [flow(wq, 0, KEYS, gp, 0, True), flow(wk, 0, KEYS, gp, KEYS, True), flow(wb, 0, LANES, gp, QKV + VALS, False)],
+        [flow(wv, 0, VALS, gp, 2 * KEYS, True)],
+        [flow(wt, 0, VALS, gp, QKV, False)],
+        [flow(wo, 0, width, go, 0, True)],
+        [flow(wd, 0, width // 2, gd, 0, True)],
+        [flow(wd, width // 2, width // 2, gd, width // 2, False)],
+        [flow(wg, 0, FF_SPLIT, gg, 0, True)],
+        [flow(wu, 0, FF_SPLIT, gu, 0, False)],
+        [flow(wg, FF_SPLIT, ff - FF_SPLIT, gg, FF_SPLIT, True)],
+        [flow(wu, FF_SPLIT, ff - FF_SPLIT, gu, FF_SPLIT, True)],
     ]
 
-    def advance(k):
-        for lag, act in ((0, "begin"), (2, "forward"), (3, "relay"), (4, "done")):
+    events = []
+    for k in range(len(stages) + 5):
+        for lag, act in ((0, "begin"), (2, "forward"), (3, "relay"), (4, "swap"), (5, "done")):
             if 0 <= k - lag < len(stages):
-                for f in stages[k - lag]:
+                events.append((act, k - lag))
+    owned = set()
+
+    def poll(count=1):
+        for _ in range(count):
+            if events:
+                act, k = events.pop(0)
+                for f in stages[k]:
+                    if act == "begin" and id(f.src_ref) not in owned:
+                        owned.add(id(f.src_ref))
+                        own_loads[[id(v) for v in shards].index(id(f.src_ref))].wait()
                     getattr(f, act)()
+
+    def until(act, k):
+        while (act, k) in events:
+            poll()
+
+    until("begin", 1)
 
     loads = {}
 
@@ -783,9 +822,6 @@
                 )
             )
             exchange[-1].start()
-        if a == 0:
-            advance(0)
-            advance(1)
         here = pl.ds(pl.multiple_of(p.s * per, 16), per)
         come[a, here, :] = sent[a, here, :]
     mine = deal[0:1, :]
@@ -836,37 +872,35 @@
         here = pl.ds(at, cols)
         load(name, gp.at[:, here], wbuf.at[:, here])
 
-    advance(2)
-    advance(3)
-    advance(4)
+    until("done", 0)
     fetch("qk", 0, 2 * KEYS)
-    advance(5)
+    fetch("bd", QKV + VALS, LANES)
+    until("done", 1)
     fetch("v", 2 * KEYS, VALS)
     loads["qk"].wait()
+    loads["bd"].wait()
     project(0, 2 * KEYS, 256)
-    advance(6)
-    fetch("gb", QKV, VALS + LANES)
+    project(QKV + VALS, LANES, LANES)
+    poll(1)
     loads["v"].wait()
     project(2 * KEYS, VALS, 256)
-    loads["gb"].wait()
-    project(QKV, VALS, 256)
-    project(QKV + VALS, LANES, LANES)
-    store.put(kept["lin"], outs["lin"])
-    steps = mixer_forward(
+    until("done", 2)
+    fetch("gate", QKV, VALS)
+    convolve, heads = mixer_forward(
         rows, offsets, lengths, kept["lin"], kept["taps"], rate, bias, gain_o, kept["act"], kept["cum"],
         kept["cum_t"], kept["tinv"], kept["fresh"], kept["heads"], mixed,
     )
-    steps[0]()
-    steps[1]()
-    advance(7)
+    convolve()
+    loads["gate"].wait()
+    project(QKV, VALS, 256)
+    store.put(kept["lin"], outs["lin"])
+    for h, head in enumerate(heads):
+        head()
+        poll(3)
+    until("done", 3)
     load("out", go, wobuf)
-    steps[2]()
-    advance(8)
-    steps[3]()
     for name in ("act", "cum", "cum_t", "tinv", "fresh", "heads"):
         store.put(kept[name], outs[name])
-    advance(9)
-    load("down", gd, wdbuf)
     loads["out"].wait()
 
     def out_step(k, carry):
@@ -883,7 +917,8 @@
     store.put(kept["normed_mid_t"], outs["normed_mid_t"])
     kept["mixed_t"][...] = transposed(mixed[...].astype(f32))
     store.put(kept["mixed_t"], outs["mixed_t"])
-    advance(10)
+    until("done", 5)
+    load("down", gd, wdbuf)
 
     def ffn(at, cols, up_at):
         def step(k, carry):
@@ -905,15 +940,17 @@
 
     low, high = pl.ds(0, FF_SPLIT), pl.ds(FF_SPLIT, ff - FF_SPLIT)
     shift = lambda s: pl.ds(ff + s.start, s.size)
+    until("done", 6)
     load("g0", gg.at[:, low], wbuf.at[:, low])
-    advance(11)
+    until("done", 7)
     load("u0", gu.at[:, low], wbuf.at[:, shift(low)])
-    advance(12)
-    load("g1", gg.at[:, high], wbuf.at[:, high])
+    poll(2)
     for name in ("down", "g0", "u0"):
         loads[name].wait()
     ffn(0, FF_SPLIT, 0)
-    advance(13)
+    until("done", 8)
+    load("g1", gg.at[:, high], wbuf.at[:, high])
+    until("done", 9)
     load("u1", gu.at[:, high], wbuf.at[:, shift(high)])
     loads["g1"].wait()
     loads["u1"].wait()
@@ -943,7 +980,7 @@
     shapes = [fn(rows, width, ff) for _, fn in FORWARD_SAVED]
     sems = pltpu.SemaphoreType.DMA
     flows = 12
-    count = flows * Flow.COUNT(n_shard // 4)
+    count = flows * Flow.count(n_shard // 4, True)
     scratch = [pltpu.VMEM(s, d) for s, d in shapes] + [
         pltpu.VMEM((n_shard, 8, rows), jnp.int32), sems((n_shard,)), sems((n_shard,)),
         pltpu.VMEM((n_shard, 16, width), bf16), sems((n_shard,)), sems((n_shard,)),
@@ -952,6 +989,7 @@
         sems((16,)), sems((count,)), sems((count,)), sems((flows,)), sems((len(shapes),)),
         pltpu.VMEM((rows, width), bf16), pltpu.VMEM((rows, VALS), bf16), pltpu.VMEM((rows, width), bf16),
     ]
+    scratch += [pltpu.VMEM(weights[k].shape, bf16) for k in (0, 1, 2, 3, 4, 5, 8, 6, 7)] + [sems((9,))]
     res = pl.pallas_call(
         functools.partial(forward_kernel, n_shard, reps),
         in_specs=[words, words] + [held] * 6 + [anywhere] * 9,
@@ -1045,16 +1083,18 @@
 
     tick.index = 0
 
-    def grad_piece(ring, size, left, right, cols, out, out_at):
+    def grad_piece(ring, size, left, right_ref, right_at, cols, out, out_at):
         def fill(piece):
+            tile = min(cols, 256)
+
             def step(t, carry):
-                c, q = t % 2, t // 2
-                here = pl.ds(pl.multiple_of(t * size, 16), size)
-                value = dot(left[here, :], right)
-                ring.own[piece.slot, q // 2, q % 2, c, pl.ds(0, size), pl.ds(0, cols)] = value.astype(bf16)
+                here = pl.ds(pl.multiple_of(t * tile, tile), tile)
+                right = right_ref[:, pl.ds(pl.multiple_of(right_at + t * tile, LANES), tile)]
+                value = dot(left[...], right).astype(bf16).reshape(ring.ys, 2, 2, size, tile)
+                ring.own[piece.slot, :, :, :, pl.ds(0, size), here] = value
                 return carry
 
-            lax.fori_loop(0, n_shard, step, 0)
+            lax.fori_loop(0, cols // tile, step, 0)
 
         tick(lambda: Piece(ring, place, size, cols, out, out_at), fill)
 
@@ -1063,21 +1103,21 @@
     def gu_piece(k):
         need("normed_mid_t", "grads_gu")
         at = k * WIDE
-        grad_piece(ring_a, rows_a, kept["normed_mid_t"], kept["grads_gu"][:, at : at + WIDE], WIDE, o_ffn, at)
+        grad_piece(ring_a, rows_a, kept["normed_mid_t"], kept["grads_gu"], at, WIDE, o_ffn, at)
 
     def down_piece(k):
         need("hidden_t", "dy")
         at = k * NARROW
-        grad_piece(ring_b, ff // n_shard, kept["hidden_t"], kept["dy"][:, at : at + NARROW], NARROW, o_down, at)
+        grad_piece(ring_b, ff // n_shard, kept["hidden_t"], kept["dy"], at, NARROW, o_down, at)
 
     def out_piece(k):
         need("mixed_t")
         at = k * NARROW
-        grad_piece(ring_b, VALS // n_shard, kept["mixed_t"], branch[:, at : at + NARROW], NARROW, o_out, at)
+        grad_piece(ring_b, VALS // n_shard, kept["mixed_t"], branch, at, NARROW, o_out, at)
 
     def proj_piece(at, cols):
         need("normed_t")
-        grad_piece(ring_a, rows_a, kept["normed_t"], lin_grad[:, at : at + cols], cols, o_proj, at)
+        grad_piece(ring_a, rows_a, kept["normed_t"], lin_grad, at, cols, o_proj, at)
 
     def gu_part(k):
         cols = pl.ds(k * FTILE, FTILE)

time: 395 us -> 361 us (0.914)
  Pallas kernels: 362 us -> 327 us
    pallas_call x1, Pallas kernels: 169 us -> 146 us  [forward_call(): pl.pallas_call(functools.partial(forward_kernel, n_shard, reps), in_specs...]
    pallas_call x1, Pallas kernels: 193 us -> 180 us  [backward_call(): pl.pallas_call(functools.partial(backward_kernel, n_shard, reps, rings, s...]
where the time goes in v3:
time: 361 us; the launch traced here: 356 us
  Pallas kernels  327 us (91%)
  local copies, waits for them, and re-layouts  19.4 us (5%)
  other arithmetic  8.84 us (2%)
    pallas_call x1, Pallas kernels, backward_call(): pl.pallas_call(functools.partial(backward_kernel, n_shard, reps, rings, s...  180 us
    pallas_call x1, Pallas kernels, forward_call(): pl.pallas_call(functools.partial(forward_kernel, n_shard, reps), in_specs...  146 us
    convert_element_type x6, other arithmetic, local(): f = lambda a: a.astype(f32)  8.14 us

profile of v3, /device:TPU:0, one launch (start us, length us, event | category | flops | bytes accessed | tf_op | source)
XLA Modules:
  0.0 356.1 jit_solution(10493930496210411021)
XLA Ops:
  0.7 1.2 pad_bitcast_fusion.1.refs_6_.refs_2_
  1.9 1.2 pad_bitcast_fusion.refs_7_.refs_3_
  3.2 0.8 dynamic_update_slice.17
  4.1 0.7 constant_dynamic-update-slice_fusion
  5.4 1.3 broadcast_in_dim.35.refs_4_
  6.7 0.7 constant_dynamic-update-slice_fusion.2
  7.5 2.0 concatenate.6.refs_5_
  9.4 0.8 copy.39
  10.2 0.8 copy.40
  11.1 0.7 maximum_maximum_fusion.refs_12_
  11.8 146.4 %shard_map.340 = (bf16[1024,4736]{1,0:T(8,128)(2,1)}, bf16[1536,1024]{1,0:T(8,128)(2,1)}, bf16[1024,2816]{1,0:T(8,128)(2,1)}, bf16[1024,2816]{1,0:T(8,128)(2,1)}...) custom-call(s32[4]{0:T(128)} %bitcast.22, ...), custom_call_target="tpu_custom_call" | custom-call | tf_op jit(solution)/shard_map/pallas_call | solution.py:993
  158.2 180.5 %shard_map.341 = (bf16[256,1024]{1,0:T(8,128)(2,1)}, bf16[256,1024]{1,0:T(8,128)(2,1)}, bf16[128,5632]{1,0:T(8,128)(2,1)}, bf16[352,1024]{1,0:T(8,128)(2,1)}, bf...) custom-call(s32[4]{0:T(128)} %bitcast.23, s32[4]{0:T(128)} %bitcast.25, ...), custom_call_target="tpu_custom_call" | custom-call | tf_op jit(solution)/shard_map/pallas_call | solution.py:1328
  338.7 0.8 slice.52
  340.1 1.3 slice_bitcast_fusion
  341.3 0.8 fusion.3
  342.7 0.9 reshape.51
  344.2 0.9 slice_convert_fusion.6
  346.4 2.0 convert_element_type.41
  348.4 0.9 slice_convert_fusion.4
  349.3 1.3 slice_convert_fusion.2
  350.6 1.3 convert_element_type.44
  352.5 1.8 slice_convert_fusion
  354.3 0.8 copy.50
  355.1 0.8 copy.51
  (26 shorter events, 4.5 us)
Async XLA Ops:
  338.7 9.7 %copy-start.1 = (bf16[128,4736]{1,0:T(8,128)(2,1)S(1)}, bf16[128,4736]{1,0:T(8,128)(2,1)}, u32[]{:S(2)}) copy-start(bf16[128,4736]{1,0:T(8,128)(2,1)} %get-tuple-element.76) | copy-start | bytes 3637252
  349.3 1.3 copy-start.2
  350.6 1.9 copy-start
  352.5 1.8 copy-start.4
  352.5 2.6 copy-start.3
